TPU v7x, 256 devices: a whole 4x4x8 slice. The times are simulated.
256 devices in a mesh: dp: 16 (over x, z_hi, core), fsdp: 16 (over y, z_lo).
Axes of the slice: x: 4, y: 4, z: 8 (z_hi: 2, z_lo: 4; z = z_hi * 4 + z_lo), core: 2. Of those that a mesh axis runs over, the one named last changes fastest.
Arguments:
- latent: bfloat16 [65536, 512], P(('dp', 'fsdp')), may hold values from -6 to 6
- cotangent: bfloat16 [65536, 16384], P(('dp', 'fsdp')), may hold values from -5 to 5
- quant: bfloat16 [512, 16384], P(None, 'fsdp'), may hold values from -6 to 6
- scales: float32 [4, 128], P(None, 'fsdp'), may hold values from 0.015 to 0.09
- adapter_down: bfloat16 [512, 64], replicated, may hold values from -0.25 to 0.25
- adapter_up: bfloat16 [64, 16384], P(None, 'fsdp'), may hold values from -0.75 to 0.75
Outputs:
- latent_gradient: bfloat16 [65536, 512], P(('dp', 'fsdp'))
- grad_a: float32 [512, 64], replicated
- grad_b: float32 [64, 16384], P(None, 'fsdp')
All inputs are finite; a program needn't handle non-finite values.
Results may differ from a plain program's by a relative error of at most 0.0049.
Values may be sent and summed in bfloat16 or wider, within the bound.
A program may use at most 128 MiB of HBM per device.

v0:
```python
import jax
import jax.numpy as jnp
from jax import lax
from jax.sharding import PartitionSpec as P

BLOCK = 128


def expand(scales):
    return jnp.repeat(jnp.repeat(scales, BLOCK, axis=0), BLOCK, axis=1)


def contract_cols(left, right):
    return lax.dot_general(
        left, right, (((1,), (1,)), ((), ())), preferred_element_type=jnp.float32
    )


def shards(latent, cotangent, quant, scales, adapter_down, adapter_up):
    weight = (quant.astype(jnp.float32) * expand(scales)).astype(jnp.bfloat16)
    lowrank_term = jnp.dot(latent, adapter_down, preferred_element_type=jnp.float32).astype(
        jnp.bfloat16
    )
    full_weight, full_up = (
        lax.all_gather(weight, "fsdp", axis=1, tiled=True),
        lax.all_gather(adapter_up, "fsdp", axis=1, tiled=True),
    )
    frozen_term = contract_cols(cotangent, full_weight)
    through_sum = contract_cols(cotangent, full_up)
    adapter_pass = through_sum.astype(jnp.bfloat16)
    latent_gradient = (
        frozen_term + jnp.dot(adapter_pass, adapter_down.T, preferred_element_type=jnp.float32)
    ).astype(jnp.bfloat16)
    term_a = jnp.dot(latent.T, adapter_pass, preferred_element_type=jnp.float32)
    term_b = jnp.dot(lowrank_term.T, cotangent, preferred_element_type=jnp.float32)
    tokens_all = cotangent.shape[0] * lax.axis_size("dp") * lax.axis_size("fsdp")
    factor = 1.0 / jnp.sqrt(jnp.float32(tokens_all))
    total_a, total_b = lax.psum((term_a, term_b), ("dp", "fsdp"))
    latent_extent = adapter_up.shape[1]
    own_b = lax.dynamic_slice_in_dim(
        total_b, lax.axis_index("fsdp") * latent_extent, latent_extent, 1
    )
    grad_a = total_a * factor
    grad_b = own_b * factor
    return (latent_gradient, grad_a, grad_b)


def solution(mesh):
    placed = (
        P(("dp", "fsdp"), None),
        P(("dp", "fsdp"), None),
        P(None, "fsdp"),
        P(None, "fsdp"),
        P(),
        P(None, "fsdp"),
    )
    return jax.shard_map(
        shards,
        mesh=mesh,
        in_specs=placed,
        out_specs=(P(("dp", "fsdp"), None), P(), P(None, "fsdp")),
        check_vma=False,
    )
```

profile of v0, /device:TPU:1, one launch (start us, length us, event | category | flops | bytes accessed | tf_op | source)
XLA Modules:
  0.0 751.3 jit_solution(14969131024986170846)
XLA Ops:
  7.2 0.0 copy-start
  7.2 0.0 all-gather.5.cloned.1.call-start
  7.2 0.7 all-gather.5.cloned.1.call-update
  7.9 0.0 all-reduce.3.cloned.1.call-start
  8.0 0.2 copy-done
  8.1 7.3 fusion.2
  15.4 0.0 copy-start.3
  15.4 0.0 copy-start.1
  15.4 76.2 %all-gather.5.cloned.1.call-done = bf16[64,16384]{1,0:T(8,128)(2,1)} async-done(((bf16[64,1024]{1,0:T(8,128)(2,1)}), bf16[64,16384]{1,0:T(8,128)(2,1)}) %all-gather.5.cloned.1.call-update) | async-done | bytes 2097168 | tf_op jit(solution)/shard_map/all_gather | solution.py:26
  91.6 6.6 convolution_convert_fusion.1
  98.2 0.8 convolution_bitcast_fusion.1
  99.0 0.0 all-reduce.3.cloned.1.call-update
  99.1 0.0 all-gather.3.cloned.1.call-start
  99.1 0.0 copy-done.3
  99.2 0.6 broadcast_in_dim.7
  99.8 0.0 copy-done.1
  99.8 1.6 fusion
  101.4 0.0 all-gather.3.cloned.1.call-update
  101.4 274.3 %all-reduce.3.cloned.1.call-done = (f32[512,64]{0,1:T(8,128)}, f32[64,16384]{1,0:T(8,128)}) async-done(((f32[512,64]{0,1:T(8,128)}, f32[64,16384]{1,0:T(8,128)}), (f32[512,64]{0,1:T(8,128)}, f32[64,16384]{1,0:T(8,128)})) %all-reduce.3.cloned.1.call-update) | async-done | bytes 4325392 | tf_op jit(solution)/shard_map/psum | solution.py:38
  375.7 1.7 dynamic-slice_multiply_fusion
  377.4 1.6 broadcast_multiply_fusion
  378.9 0.0 copy-start.2
  378.9 354.1 %all-gather.3.cloned.1.call-done = bf16[512,16384]{1,0:T(8,128)(2,1)} async-done(((bf16[512,1024]{1,0:T(8,128)(2,1)}), bf16[512,16384]{1,0:T(8,128)(2,1)}) %all-gather.3.cloned.1.call-update) | async-done | bytes 16777232 | tf_op jit(solution)/shard_map/all_gather | solution.py:25
  733.1 10.5 %convolution_bitcast_fusion = f32[256,512]{0,1:T(8,128)S(1)} fusion(bf16[512,16384]{1,0:T(8,128)(2,1)} %all-gather.3.cloned.1.call-done, bf16[256,16384]{1,0:T(8,128)(2,1)} %param.7), kind=kOutput, calls=%fused_computation.3 | convolution fusion | flops 4294967296 | bytes 25690112 | tf_op jit(solution)/shard_map/dot_general | solution.py:14
  743.6 0.0 copy-done.2
  743.6 0.3 fusion.1
  743.9 0.8 copy.10
  (1 shorter events, 0.0 us)
Async XLA Ops:
  7.2 1.0 copy-start
  7.2 84.4 %all-gather.5.cloned.1.call-start = ((), (), s32[]{:S(2)}) async-start(), calls=%async_computation.1 | async-start | bytes 2228224 | tf_op jit(solution)/shard_map/all_gather | solution.py:26
  7.9 367.8 %all-reduce.3.cloned.1.call-start = ((), (), s32[]{:S(2)}) async-start(), calls=%async_computation.2 | async-start | bytes 8650752 | tf_op jit(solution)/shard_map/psum | solution.py:38
  15.4 83.7 %copy-start.3 = (f32[4,8]{1,0:T(4,128)S(1)}, f32[4,8]{1,0:T(4,128)}, u32[]{:S(2)}) copy-start(f32[4,8]{1,0:T(4,128)} %param.9) | copy-start | bytes 388
  15.4 84.3 %copy-start.1 = (bf16[512,1024]{1,0:T(8,128)(2,1)S(1)}, bf16[512,1024]{1,0:T(8,128)(2,1)}, u32[]{:S(2)}) copy-start(bf16[512,1024]{1,0:T(8,128)(2,1)} %param.8) | copy-start | bytes 3145732
  99.1 634.0 %all-gather.3.cloned.1.call-start = ((), (), s32[]{:S(2)}) async-start(), calls=%async_computation | async-start | bytes 17825792 | tf_op jit(solution)/shard_map/all_gather | solution.py:25
  378.9 364.7 %copy-start.2 = (bf16[512,64]{0,1:T(8,128)(2,1)S(1)}, bf16[512,64]{0,1:T(8,128)(2,1)}, u32[]{:S(2)}) copy-start(bf16[512,64]{0,1:T(8,128)(2,1)} %param.10) | copy-start | bytes 196612
Sparse Core Ops, SparseCore 0:
  9.8 81.7 all-gather.4
  99.2 276.4 all-reduce.2
  377.6 355.3 all-gather.2
where the time goes:
time: 751 us
  waiting for transfers between devices  705 us (94%)
  matrix products  25.5 us (3%)
  between operations  13.8 us (2%)
    all_gather x1, waiting for transfers between devices, shards(): lax.all_gather(weight, 'fsdp', axis=1, tiled=True)  354 us
    psum x1, waiting for transfers between devices, shards(): total_a, total_b = lax.psum((term_a, term_b), ('dp', 'fsdp'))  274 us
    all_gather x1, waiting for transfers between devices, shards(): lax.all_gather(adapter_up, 'fsdp', axis=1, tiled=True)  76.2 us
    dot_general x2, matrix products, contract_cols(): lax.dot_general(left, right, (((1,), (1,)), ((), ())), preferred_element_...  17.2 us
  transfers between devices with their start and end apart: 3, of which 3 were waited for; matrix products, arithmetic and copies ran while one was open for 2% of the time, Pallas kernels for 0%

commit v1 on v0

v1 whole, which is shorter than its diff:
```python
import jax
import jax.numpy as jnp
from jax import lax
from jax.experimental import pallas as pl
from jax.experimental.pallas import tpu as pltpu
from jax.sharding import PartitionSpec as P

MESH = pl.DeviceIdType.MESH
BLOCK = 128
NX, NY, NZ, NC = 4, 4, 8, 2
NS = 4
TOK, COLS, LAT, RANK = 256, 16384, 512, 64
SHARD = COLS // (NY * NS)
QUART = SHARD // 4
HALF = RANK // 2
EXCL = 128
FETCH = LAT - EXCL
TOTAL = 65536
GROUPS = 4

SENDS = 224
RECVS = 224

ORDER = [
    (-1, 0), (1, 0), (0, -1), (0, 1), (2, 0),
    (-1, -1), (-1, 1), (1, -1), (1, 1),
    (0, 2), (2, -1), (2, 1), (-1, 2), (1, 2), (2, 2),
]


def dot_cols(left, right):
    return lax.dot_general(
        left, right, (((1,), (1,)), ((), ())), preferred_element_type=jnp.float32
    )


def kernel(
    scales, latent, cot_hbm, quant, down, up,
    out_lat, out_a, out_b,
    cot, wbuf, ubuf, low_t, acc, thr, own, sib_out, sib_in, x_out, x_in, y_own, y_in,
    z_own, z_in, gath, a_own, a_in, ay_own, ay_in, az_in, ay_all, a_all,
    load_sem, send_sem, recv_sem,
):
    d, f = lax.axis_index("dp"), lax.axis_index("fsdp")
    x, c = lax.div(d, 4), lax.rem(d, 2)
    y, zl = lax.div(f, 4), lax.rem(f, 4)
    z = lax.rem(lax.div(d, 2), 2) * 4 + zl
    par = lax.rem(x, 2)
    me8 = x * 2 + c

    def dev(xx, yy, zz, cc):
        return (xx * 4 + lax.div(zz, 4) * 2 + cc, yy * 4 + lax.rem(zz, 4))

    def at_x(k):
        return dev(lax.rem(x + k + NX, NX), y, z, c)

    def at_y(k):
        return dev(x, lax.rem(y + k + NY, NY), z, c)

    def at_z(k):
        return dev(x, y, lax.rem(z + k + NZ, NZ), c)

    def at_8(k):
        p = lax.rem(me8 + k, 8)
        return dev(lax.div(p, 2), y, z, lax.rem(p, 2))

    sibling = dev(x, y, z, 1 - c)

    sent = []
    events = {}

    def event(name):
        return recv_sem.at[events.setdefault(name, len(events))]

    def send(name, src, dst, target):
        copy = pltpu.make_async_remote_copy(
            src_ref=src, dst_ref=dst, send_sem=send_sem.at[len(sent)],
            recv_sem=event(name), device_id=target, device_id_type=MESH,
        )
        copy.start()
        sent.append(copy)

    def arrived(name, dst):
        pltpu.make_async_remote_copy(
            src_ref=dst, dst_ref=dst, send_sem=send_sem.at[0],
            recv_sem=event(name), device_id=sibling, device_id_type=MESH,
        ).wait_recv()

    wide = COLS // GROUPS
    loads = []
    for g in range(GROUPS):
        cols = pl.ds(g * wide, wide)
        copy = pltpu.make_async_copy(cot_hbm.at[:, cols], cot.at[:, cols], load_sem.at[g])
        copy.start()
        loads.append(copy)
    barrier = pltpu.get_barrier_semaphore()
    partners = (
        [at_8(k) for k in range(1, 8)]
        + [at_y(k) for k in range(1, NY)]
        + [at_z(k) for k in range(1, NZ)]
    )
    for partner in partners:
        pl.semaphore_signal(barrier, inc=1, device_id=partner, device_id_type=MESH)

    for q in range(4):
        ubuf[q, y, zl] = up[:, q * QUART:(q + 1) * QUART]
        for i in range(LAT // BLOCK):
            for j in range(QUART // BLOCK):
                col = q * QUART + j * BLOCK
                block = quant[i * BLOCK:(i + 1) * BLOCK, col:col + BLOCK].astype(jnp.float32)
                wbuf[q, y, zl, i * BLOCK:(i + 1) * BLOCK, j * BLOCK:(j + 1) * BLOCK] = (
                    block * scales[i, col // BLOCK]
                ).astype(jnp.bfloat16)
    pl.semaphore_wait(barrier, len(partners))

    def slot(j, da, db):
        dy, dz = (da, db) if j == 0 else (db, da)
        return lax.rem(y + dy + NY, NY), lax.rem(zl + dz + NS, NS)

    def along(j, axis, step):
        return at_y(step) if (j == 0) == (axis == 0) else at_z(step)

    def up_ref(j, da, db, core=None):
        ys, zs = slot(j, da, db)
        return ubuf.at[2 * (c if core is None else core) + j, ys, zs]

    def w_ref(j, da, db, part="fetch", core=None):
        ys, zs = slot(j, da, db)
        ref = wbuf.at[2 * (c if core is None else core) + j, ys, zs]
        low = par * EXCL
        if part == "fetch":
            return ref.at[pl.ds(low, FETCH)]
        if part == "h0":
            return ref.at[pl.ds(low, FETCH // 2)]
        if part == "h1":
            return ref.at[pl.ds(low + FETCH // 2, FETCH // 2)]
        if part == "mine":
            return ref.at[pl.ds(par * FETCH, EXCL)]
        if part == "missing":
            return ref.at[pl.ds((1 - par) * FETCH, EXCL)]
        return ref

    def pass_up(j, da):
        for step, name in ((1, -1), (-1, 1), (2, 2)):
            ref = up_ref(j, da, 0)
            send(("u", j, da, name), ref, ref, along(j, 1, step))

    def up_start():
        for j in (0, 1):
            own_up = up_ref(j, 0, 0)
            for step, name in ((1, -1), (-1, 1), (2, 2)):
                send(("u", j, name, 0), own_up, own_up, along(j, 0, step))
        for j in (0, 1):
            pass_up(j, 0)

    def up_first(da):
        for j in (0, 1):
            arrived(("u", j, da, 0), up_ref(j, da, 0))
            pass_up(j, da)

    def up_share():
        for j in (0, 1):
            for da in (0, -1, 1, 2):
                for db in (-1, 1, 2):
                    arrived(("u", j, da, db), up_ref(j, da, db))
            ref = ubuf.at[2 * c + j]
            send(("us", j), ref, ref, sibling)

    def up_finish():
        for j in (0, 1):
            arrived(("us", j), ubuf.at[2 * (1 - c) + j])

    def w_second(j, da):
        ref = w_ref(j, da, 0)
        send(("w", j, da, -1), ref, ref, along(j, 1, 1))
        send(("w", j, da, 1), ref, ref, along(j, 1, -1))

    def w_start():
        for j in (0, 1):
            ref = w_ref(j, 0, 0)
            send(("w", j, -1, 0), ref, ref, along(j, 0, 1))
            send(("w", j, 1, 0), ref, ref, along(j, 0, -1))
        for j in (0, 1):
            w_second(j, 0)

    def w_take(j, da, db):
        if 2 in (da, db) and (db == 2 or db == 0):
            arrived(("w", j, da, db, 0), w_ref(j, da, db, "h0"))
            arrived(("w", j, da, db, 1), w_ref(j, da, db, "h1"))
        else:
            arrived(("w", j, da, db), w_ref(j, da, db))
        axis, o = (0, da) if db == 0 else (1, db)
        if o in (-1, 1):
            ref = w_ref(j, da, db, "h0" if o == -1 else "h1")
            name = ("w", j, 2, 0) if axis == 0 else ("w", j, da, 2)
            send(name + (0 if o == -1 else 1,), ref, ref, along(j, axis, -o))
        if db == 0:
            w_second(j, da)
        ref = w_ref(j, da, db, "mine")
        send(("wx", j, da, db), ref, ref, at_x(1 if j == 0 else -1))

    def w_share(j, da, db):
        arrived(("wx", j, da, db), w_ref(j, da, db, "missing"))
        ref = w_ref(j, da, db, "all")
        send(("ws", j, da, db), ref, ref, sibling)

    def w_use(j, da, db, wait=True):
        if wait:
            arrived(("ws", j, da, db), w_ref(j, da, db, "all", 1 - c))
        ys, zs = slot(j, da, db)
        total = None
        for core in (0, 1):
            q = 2 * core + j
            base = pl.multiple_of((ys * NS + zs) * SHARD + q * QUART, QUART)
            term = dot_cols(cot[:, pl.ds(base, QUART)], wbuf[q, ys, zs])
            total = term if total is None else total + term
        acc[...] += total

    def b_terms(g):
        loads[g].wait()
        for s in range(g * GROUPS, (g + 1) * GROUPS):
            term = jnp.dot(
                low_t[...], cot[:, s * SHARD:(s + 1) * SHARD],
                preferred_element_type=jnp.float32,
            )
            own[s] = jnp.where(c == 0, term[:HALF], term[HALF:])
            sib_out[s] = jnp.where(c == 0, term[HALF:], term[:HALF]).astype(jnp.bfloat16)
        part = pl.ds(g * GROUPS, GROUPS)
        send(("b0", g), sib_out.at[part], sib_in.at[part], sibling)

    def b_cores(g):
        part = pl.ds(g * GROUPS, GROUPS)
        arrived(("b0", g), sib_in.at[part])
        for s in range(g * GROUPS, (g + 1) * GROUPS):
            total = own[s] + sib_in[s].astype(jnp.float32)
            own[s] = total
            for k in range(NX):
                x_out[k, s] = total[:, k * QUART:(k + 1) * QUART].astype(jnp.bfloat16)

    def b_x_send():
        for k in (1, 3, 2):
            send(("b1", k), x_out.at[lax.rem(x + k, NX)], x_in.at[k - 1], at_x(k))

    def b_x_sum():
        for k in (1, 3, 2):
            arrived(("b1", k), x_in.at[k - 1])
        mine = pl.ds(pl.multiple_of(x * QUART, QUART), QUART)
        for yy in range(NY):
            for zz in range(NS):
                s = yy * NS + zz
                total = own[s, :, mine]
                for k in range(NX - 1):
                    total = total + x_in[k, s].astype(jnp.float32)
                y_own[yy, zz] = total
        for k in (1, 3, 2):
            send(("b2", k), y_own.at[lax.rem(y + k, NY)], y_in.at[k - 1], at_y(k))

    def b_y_sum():
        for k in (1, 3, 2):
            arrived(("b2", k), y_in.at[k - 1])
        for zz in range(NS):
            total = y_own[y, zz]
            for k in range(NY - 1):
                total = total + y_in[k, zz]
            z_own[zz] = total
        z_in[z] = z_own[zl]
        for k in range(1, NZ):
            send(("b3", k), z_own.at[lax.rem(zl + k, NS)], z_in.at[z], at_z(k))

    def b_z_sum():
        for k in range(1, NZ):
            arrived(("b3", k), z_in.at[lax.rem(z + NZ - k, NZ)])
        total = z_in[0]
        for k in range(1, NZ):
            total = total + z_in[k]
        gath[me8] = total * (1.0 / TOTAL ** 0.5)
        for k in range(1, 8):
            send(("b4", k), gath.at[me8], gath.at[me8], at_8(k))

    def b_write():
        for k in range(1, 8):
            arrived(("b4", k), gath.at[lax.rem(me8 + 8 - k, 8)])
        for p in range(8):
            rows, cols = (p % 2) * HALF, (p // 2) * QUART
            out_b[rows:rows + HALF, cols:cols + QUART] = gath[p]

    def a_terms():
        def step(s, total):
            for q in range(4):
                base = pl.multiple_of(s * SHARD + q * QUART, QUART)
                total = total + dot_cols(
                    cot[:, pl.ds(base, QUART)], ubuf[q, lax.div(s, NS), lax.rem(s, NS)]
                )
            return total

        through = lax.fori_loop(0, NY * NS, step, jnp.zeros((TOK, RANK), jnp.float32))
        thr[...] = through.astype(jnp.bfloat16)
        through_t = through.astype(jnp.bfloat16).astype(jnp.float32).T.astype(jnp.bfloat16)
        term = jnp.dot(through_t, latent[...], preferred_element_type=jnp.float32)
        for p in range(8):
            a_own[p] = term[p * 8:(p + 1) * 8]
        for k in range(1, 8):
            send(("a1", k), a_own.at[lax.rem(me8 + k, 8)], a_in.at[k - 1], at_8(k))

    def a_8_sum():
        for k in range(1, 8):
            arrived(("a1", k), a_in.at[k - 1])
        total = a_own[me8]
        for k in range(7):
            total = total + a_in[k]
        for yy in range(NY):
            ay_own[yy] = total[:, yy * BLOCK:(yy + 1) * BLOCK]
        for k in (1, 3, 2):
            send(("a2", k), ay_own.at[lax.rem(y + k, NY)], ay_in.at[k - 1], at_y(k))

    def a_y_sum():
        for k in (1, 3, 2):
            arrived(("a2", k), ay_in.at[k - 1])
        total = ay_own[y]
        for k in range(NY - 1):
            total = total + ay_in[k]
        az_in[z] = total
        for k in range(1, NZ):
            send(("a3", k), az_in.at[z], az_in.at[z], at_z(k))

    def a_z_sum():
        for k in range(1, NZ):
            arrived(("a3", k), az_in.at[lax.rem(z + NZ - k, NZ)])
        total = az_in[0]
        for k in range(1, NZ):
            total = total + az_in[k]
        ay_all[y] = total * (1.0 / TOTAL ** 0.5)
        for k in (1, 3, 2):
            send(("a4", k), ay_all.at[y], ay_all.at[y], at_y(k))

    def a_spread():
        for k in (1, 3, 2):
            arrived(("a4", k), ay_all.at[lax.rem(y + NY - k, NY)])
        for yy in range(NY):
            a_all[me8, :, yy * BLOCK:(yy + 1) * BLOCK] = ay_all[yy]
        for k in range(1, 8):
            send(("a5", k), a_all.at[me8], a_all.at[me8], at_8(k))

    def a_write():
        for k in range(1, 8):
            arrived(("a5", k), a_all.at[lax.rem(me8 + 8 - k, 8)])
        for p in range(8):
            out_a[p * 8:(p + 1) * 8] = a_all[p]

    up_start()
    w_start()
    acc[...] = jnp.zeros_like(acc)
    low = jnp.dot(latent[...], down[...], preferred_element_type=jnp.float32)
    low_t[...] = low.astype(jnp.bfloat16).astype(jnp.float32).T.astype(jnp.bfloat16)
    b_terms(0)
    up_first(-1)
    up_first(1)
    b_terms(1)
    up_first(2)
    b_terms(2)
    b_cores(0)
    b_terms(3)
    for g in range(1, GROUPS):
        b_cores(g)
    b_x_send()

    items = [(j, da, db) for da, db in ORDER for j in (0, 1)]
    extra = {
        0: [lambda: w_use(0, 0, 0, False), lambda: w_use(1, 0, 0, False)],
        4: [up_share],
        8: [up_finish, a_terms],
        11: [b_x_sum],
        14: [a_8_sum],
        16: [b_y_sum],
        18: [a_y_sum],
        20: [b_z_sum],
        23: [a_z_sum],
        27: [a_spread],
        28: [b_write],
    }
    lag_x, lag_s = 3, 6
    for i in range(len(items) + lag_s):
        if i < len(items):
            w_take(*items[i])
        if 0 <= i - lag_x < len(items):
            w_share(*items[i - lag_x])
        if 0 <= i - lag_s < len(items):
            w_use(*items[i - lag_s])
        for task in extra.get(i, ()):
            task()
    out_lat[...] = (acc[...] + dot_cols(thr[...], down[...])).astype(jnp.bfloat16)
    a_write()
    for copy in sent:
        copy.wait_send()


def shards(latent, cotangent, quant, scales, adapter_down, adapter_up):
    vmem = pl.BlockSpec(memory_space=pltpu.VMEM)
    bf16, f32 = jnp.bfloat16, jnp.float32
    lat, grad_a_t, grad_b = pl.pallas_call(
        kernel,
        name="adapter_backward",
        out_shape=(
            jax.ShapeDtypeStruct((TOK, LAT), bf16),
            jax.ShapeDtypeStruct((RANK, LAT), f32),
            jax.ShapeDtypeStruct((RANK, SHARD), f32),
        ),
        in_specs=[
            pl.BlockSpec(memory_space=pltpu.SMEM), vmem,
            pl.BlockSpec(memory_space=pl.ANY), vmem, vmem, vmem,
        ],
        out_specs=(vmem, vmem, vmem),
        scratch_shapes=[
            pltpu.VMEM((TOK, COLS), bf16),
            pltpu.VMEM((4, NY, NS, LAT, QUART), bf16),
            pltpu.VMEM((4, NY, NS, RANK, QUART), bf16),
            pltpu.VMEM((RANK, TOK), bf16),
            pltpu.VMEM((TOK, LAT), f32),
            pltpu.VMEM((TOK, RANK), bf16),
            pltpu.VMEM((NY * NS, HALF, SHARD), f32),
            pltpu.VMEM((NY * NS, HALF, SHARD), bf16),
            pltpu.VMEM((NY * NS, HALF, SHARD), bf16),
            pltpu.VMEM((NX, NY * NS, HALF, QUART), bf16),
            pltpu.VMEM((NX - 1, NY * NS, HALF, QUART), bf16),
            pltpu.VMEM((NY, NS, HALF, QUART), f32),
            pltpu.VMEM((NY - 1, NS, HALF, QUART), f32),
            pltpu.VMEM((NS, HALF, QUART), f32),
            pltpu.VMEM((NZ, HALF, QUART), f32),
            pltpu.VMEM((8, HALF, QUART), f32),
            pltpu.VMEM((8, 8, LAT), f32),
            pltpu.VMEM((7, 8, LAT), f32),
            pltpu.VMEM((NY, 8, BLOCK), f32),
            pltpu.VMEM((NY - 1, 8, BLOCK), f32),
            pltpu.VMEM((NZ, 8, BLOCK), f32),
            pltpu.VMEM((NY, 8, BLOCK), f32),
            pltpu.VMEM((8, 8, LAT), f32),
            pltpu.SemaphoreType.DMA((GROUPS,)),
            pltpu.SemaphoreType.DMA((SENDS,)),
            pltpu.SemaphoreType.DMA((RECVS,)),
        ],
        compiler_params=pltpu.CompilerParams(
            collective_id=0, has_side_effects=True, vmem_limit_bytes=56 * 2**20
        ),
        cost_estimate=pl.CostEstimate(
            flops=2 * TOK * COLS * (LAT + 2 * RANK), bytes_accessed=12 * 2**20, transcendentals=0
        ),
    )(scales, latent, cotangent, quant, adapter_down, adapter_up)
    return lat, grad_a_t.T, grad_b


def solution(mesh):
    placed = (
        P(("dp", "fsdp"), None),
        P(("dp", "fsdp"), None),
        P(None, "fsdp"),
        P(None, "fsdp"),
        P(),
        P(None, "fsdp"),
    )
    return jax.shard_map(
        shards,
        mesh=mesh,
        in_specs=placed,
        out_specs=(P(("dp", "fsdp"), None), P(), P(None, "fsdp")),
        check_vma=False,
    )
```

time: 751 us -> 95.6 us (0.13)
  waiting for transfers between devices: 705 us -> 0 us
  Pallas kernels: 0 us -> 87.9 us
  matrix products: 25.5 us -> 0 us
  between operations: 13.8 us -> 0.64 us
    all_gather x2 -> x0, waiting for transfers between devices: 430 us -> none  [the longest x1 354 us: shards(): lax.all_gather(weight, 'fsdp', axis=1, tiled=True)]
    psum x1 -> x0, waiting for transfers between devices: 274 us -> none  [shards(): total_a, total_b = lax.psum((term_a, term_b), ('dp', 'fsdp'))]
    pallas_call x0 -> x1, Pallas kernels: none -> 87.9 us  [shards(): pl.pallas_call(kernel, name='adapter_backward', out_shape=(jax.ShapeDtype...]
    dot_general x5 -> x0, matrix products: 25.5 us -> none  [the longest x2 17.2 us: contract_cols(): lax.dot_general(left, right, (((1,), (1,)), ((), ())), preferred_element_...]
  transfers between devices with their start and end apart: 3 -> 0, of which waited for: 3 -> 0; matrix products, arithmetic and copies ran while one was open for 2% -> 0% of each run, Pallas kernels for 0% -> 0%
where the time goes in v1:
time: 95.6 us; the launch traced here: 95 us
  Pallas kernels  87.9 us (92%)
  local copies, waits for them, and re-layouts  6.51 us (7%)
    pallas_call x1, Pallas kernels, shards(): pl.pallas_call(kernel, name='adapter_backward', out_shape=(jax.ShapeDtype...  87.9 us
    unnamed x4, local copies, waits for them, and re-layouts  6.51 us

profile of v1, /device:TPU:1, one launch (start us, length us, event | category | flops | bytes accessed | tf_op | source)
XLA Modules:
  0.0 95.0 jit_solution(649358707081606646)
XLA Ops:
  0.6 1.6 %copy.9.down = bf16[512,64]{1,0:T(8,128)(2,1)} copy(bf16[512,64]{0,1:T(8,128)(2,1)} %param.10) | data formatting | bytes 131072 | tf_op args[4]
  2.2 87.9 %adapter_backward.1 = (bf16[256,512]{1,0:T(8,128)(2,1)}, f32[64,512]{1,0:T(8,128)}, f32[64,1024]{1,0:T(8,128)}) custom-call(f32[4,8]{1,0:T(4,128)} %scales.1, bf16[256,512]{1,0:T(8,128)(2,1)} %latent.1, bf16[256,16384]{1,0:T(8,128)(2,1)} %cot_hbm.1, bf16[512,1024]{1,0:T(8,128)(2,1)} %quant.1, bf16[512,64]{1,0:T(8,128)(2,1)} %copy.9.down, bf16[64,1024]{1,0:T(8,128)(2,1)} %up.1), custom_call_target="tpu_custom_call" | custom-call | flops 5368709120 | bytes 12582912 | tf_op jit(solution)/shard_map/adapter_backward/pallas_call | solution.py:400
  90.1 1.7 %copy.13 = bf16[256,512]{1,0:T(8,128)(2,1)} copy(bf16[256,512]{1,0:T(8,128)(2,1)} %get-tuple-element.12) | data formatting | bytes 524288
  91.8 1.6 %copy.14 = f32[512,64]{0,1:T(8,128)} copy(f32[512,64]{0,1:T(8,128)} %bitcast.1) | data formatting | bytes 262144
  93.4 1.7 %copy.15 = f32[64,1024]{1,0:T(8,128)} copy(f32[64,1024]{1,0:T(8,128)} %get-tuple-element.14) | data formatting | bytes 524288

commit v2 on v1

v2 whole, which is shorter than its diff:
```python
import jax
import jax.numpy as jnp
from jax import lax
from jax.experimental import pallas as pl
from jax.experimental.pallas import tpu as pltpu
from jax.sharding import PartitionSpec as P

MESH = pl.DeviceIdType.MESH
BLOCK = 128
NX, NY, NZ = 4, 4, 8
NS = 4
TOK, COLS, LAT, RANK = 256, 16384, 512, 64
SHARD = COLS // (NY * NS)
CORE = SHARD // 2
UNIT = CORE // 2
SHARDS = NY * NS
MINE = COLS // 2
CHIP = 2 * TOK
PIECE = RANK // NX
EXCL = 144
FETCH = LAT - EXCL
HALF0 = FETCH // 32 * 16
FACTOR = 1.0 / 65536.0 ** 0.5
SENDS = 192
RECVS = 192

ORDER = [
    (-1, 0), (1, 0), (0, -1), (0, 1), (2, 0),
    (-1, -1), (-1, 1), (1, -1), (1, 1),
    (0, 2), (2, -1), (2, 1), (-1, 2), (1, 2), (2, 2),
]


def dot_cols(left, right):
    return lax.dot_general(
        left, right, (((1,), (1,)), ((), ())), preferred_element_type=jnp.float32
    )


def kernel(
    scales, latent_hbm, cot_hbm, quant_hbm, down_hbm, up_hbm,
    out_lat, out_a, out_b,
    latent, down, quant, cot, wbuf, ubuf, low_t, acc, acc_in, thr, thr_in, own, x_out, x_in,
    y_own, y_out, y_in, z_own, z_in, gath,
    a_own, a_in, ay_in, az_in, a_all,
    load_sem, send_sem, recv_sem,
):
    d, f = lax.axis_index("dp"), lax.axis_index("fsdp")
    x, c = lax.div(d, 4), lax.rem(d, 2)
    y, zl = lax.div(f, 4), lax.rem(f, 4)
    z = lax.rem(lax.div(d, 2), 2) * 4 + zl
    par = lax.rem(x, 2)
    me8 = x * 2 + c

    def dev(xx, yy, zz, cc):
        return (xx * 4 + lax.div(zz, 4) * 2 + cc, yy * 4 + lax.rem(zz, 4))

    def at_x(k):
        return dev(lax.rem(x + k + NX, NX), y, z, c)

    def at_y(k):
        return dev(x, lax.rem(y + k + NY, NY), z, c)

    def at_z(k):
        return dev(x, y, lax.rem(z + k + NZ, NZ), c)

    def at_8(k):
        p = lax.rem(me8 + k, 8)
        return dev(lax.div(p, 2), y, z, lax.rem(p, 2))

    sibling = dev(x, y, z, 1 - c)

    sent = []
    events = {}

    def event(name):
        return recv_sem.at[events.setdefault(name, len(events))]

    def send(name, src, dst, target):
        copy = pltpu.make_async_remote_copy(
            src_ref=src, dst_ref=dst, send_sem=send_sem.at[len(sent)],
            recv_sem=event(name), device_id=target, device_id_type=MESH,
        )
        copy.start()
        sent.append(copy)

    def arrived(name, dst):
        pltpu.make_async_remote_copy(
            src_ref=dst, dst_ref=dst, send_sem=send_sem.at[0],
            recv_sem=event(name), device_id=sibling, device_id_type=MESH,
        ).wait_recv()

    barrier = pltpu.get_barrier_semaphore()
    partners = (
        [at_8(k) for k in range(1, 8)]
        + [at_y(k) for k in range(1, NY)]
        + [at_z(k) for k in range(1, NZ)]
    )
    for partner in partners:
        pl.semaphore_signal(barrier, inc=1, device_id=partner, device_id_type=MESH)

    loads = {}

    def load(name, src, dst):
        copy = pltpu.make_async_copy(src, dst, load_sem.at[len(loads)])
        copy.start()
        loads[name] = copy

    half = pl.multiple_of(c * CORE, CORE)
    tokens = pl.ds(pl.multiple_of(c * TOK, TOK), TOK)
    others = pl.ds(pl.multiple_of((1 - c) * TOK, TOK), TOK)
    for j in (0, 1):
        load(("up", j), up_hbm.at[:, pl.ds(half + j * UNIT, UNIT)], ubuf.at[j, y, zl])
    load("quant", quant_hbm.at[:, pl.ds(half, CORE)], quant)
    load("latent", latent_hbm, latent)
    load("down", down_hbm, down)
    for s in range(SHARDS):
        load(
            ("cot", s), cot_hbm.at[:, pl.ds(s * SHARD + half, CORE)],
            cot.at[tokens, pl.ds(s * CORE, CORE)],
        )

    def slot(j, da, db):
        dy, dz = (da, db) if j == 0 else (db, da)
        return lax.rem(y + dy + NY, NY), lax.rem(zl + dz + NS, NS)

    def along(j, axis, step):
        return at_y(step) if (j == 0) == (axis == 0) else at_z(step)

    def up_ref(j, da, db):
        ys, zs = slot(j, da, db)
        return ubuf.at[j, ys, zs]

    def w_ref(j, da, db, part="fetch"):
        ys, zs = slot(j, da, db)
        ref = wbuf.at[j, ys, zs]
        low = par * EXCL
        if part == "fetch":
            return ref.at[pl.ds(low, FETCH)]
        if part == "h0":
            return ref.at[pl.ds(low, HALF0)]
        if part == "h1":
            return ref.at[pl.ds(low + HALF0, FETCH - HALF0)]
        if part == "mine":
            return ref.at[pl.ds(par * FETCH, EXCL)]
        return ref.at[pl.ds((1 - par) * FETCH, EXCL)]

    def pass_up(j, da):
        for step, name in ((1, -1), (-1, 1), (2, 2)):
            ref = up_ref(j, da, 0)
            send(("u", j, da, name), ref, ref, along(j, 1, step))

    def up_start():
        for j in (0, 1):
            own_up = up_ref(j, 0, 0)
            for step, name in ((1, -1), (-1, 1), (2, 2)):
                send(("u", j, name, 0), own_up, own_up, along(j, 0, step))
        for j in (0, 1):
            pass_up(j, 0)

    def up_first(da):
        for j in (0, 1):
            arrived(("u", j, da, 0), up_ref(j, da, 0))
            pass_up(j, da)

    def up_all():
        for j in (0, 1):
            for da in (0, -1, 1, 2):
                for db in (-1, 1, 2):
                    arrived(("u", j, da, db), up_ref(j, da, db))

    def w_second(j, da):
        ref = w_ref(j, da, 0)
        send(("w", j, da, -1), ref, ref, along(j, 1, 1))
        send(("w", j, da, 1), ref, ref, along(j, 1, -1))

    def w_start(j):
        for i in range(LAT // BLOCK):
            for k in range(UNIT // BLOCK):
                col = j * UNIT + k * BLOCK
                block = quant[i * BLOCK:(i + 1) * BLOCK, col:col + BLOCK].astype(jnp.float32)
                wbuf[j, y, zl, i * BLOCK:(i + 1) * BLOCK, k * BLOCK:(k + 1) * BLOCK] = (
                    block * scales[i, c * (CORE // BLOCK) + col // BLOCK]
                ).astype(jnp.bfloat16)
        ref = w_ref(j, 0, 0)
        send(("w", j, -1, 0), ref, ref, along(j, 0, 1))
        send(("w", j, 1, 0), ref, ref, along(j, 0, -1))

    def w_take(j, da, db):
        if db == 2 or (da, db) == (2, 0):
            arrived(("w", j, da, db, 0), w_ref(j, da, db, "h0"))
            arrived(("w", j, da, db, 1), w_ref(j, da, db, "h1"))
        else:
            arrived(("w", j, da, db), w_ref(j, da, db))
        axis, o = (0, da) if db == 0 else (1, db)
        if o in (-1, 1):
            ref = w_ref(j, da, db, "h0" if o == -1 else "h1")
            name = ("w", j, 2, 0) if axis == 0 else ("w", j, da, 2)
            send(name + (0 if o == -1 else 1,), ref, ref, along(j, axis, -o))
        ref = w_ref(j, da, db, "mine")
        send(("wx", j, da, db), ref, ref, at_x(1 if j == 0 else -1))

    def w_ready(da, db):
        for j in (0, 1):
            arrived(("wx", j, da, db), w_ref(j, da, db, "missing"))

    def w_use(da, db, rows=slice(None)):
        total = None
        for j in (0, 1):
            ys, zs = slot(j, da, db)
            base = pl.multiple_of((ys * NS + zs) * CORE + j * UNIT, UNIT)
            term = dot_cols(cot[rows, pl.ds(base, UNIT)], wbuf[j, ys, zs])
            total = term if total is None else total + term
        if (da, db) == (0, 0):
            acc[...] = total
        else:
            acc[rows] += total

    def low_start():
        loads["latent"].wait()
        loads["down"].wait()
        low = jnp.dot(
            latent[...], down[...].astype(jnp.float32).T.astype(jnp.bfloat16),
            preferred_element_type=jnp.float32,
        )
        low_t[c] = low.astype(jnp.bfloat16).astype(jnp.float32).T.astype(jnp.bfloat16)
        send("low", low_t.at[c], low_t.at[c], sibling)

    def cot_send():
        for s in range(SHARDS):
            send(
                ("cot", s), cot_hbm.at[:, pl.ds(s * SHARD + CORE - half, CORE)],
                cot.at[tokens, pl.ds(s * CORE, CORE)], sibling,
            )

    def cot_wait(s):
        loads["cot", s].wait()
        arrived(("cot", s), cot.at[others, pl.ds(s * CORE, CORE)])

    def b_terms(g):
        if g == 0:
            arrived("low", low_t.at[1 - c])
        for s in range(g * NS, (g + 1) * NS):
            cot_wait(s)
            cols = slice(s * CORE, (s + 1) * CORE)
            term = jnp.dot(low_t[0], cot[:TOK, cols], preferred_element_type=jnp.float32)
            term += jnp.dot(low_t[1], cot[TOK:, cols], preferred_element_type=jnp.float32)
            own[s] = term
            for k in range(NX):
                x_out[k, s] = term[k * PIECE:(k + 1) * PIECE].astype(jnp.bfloat16)
        part = pl.ds(g * NS, NS)
        for k in (1, 3, 2):
            send(
                ("b1", k, g), x_out.at[lax.rem(x + k, NX), part], x_in.at[k - 1, part], at_x(k)
            )

    def b_x_sum():
        mine = pl.ds(pl.multiple_of(x * PIECE, PIECE), PIECE)
        for g in range(NY):
            for k in (1, 3, 2):
                arrived(("b1", k, g), x_in.at[k - 1, pl.ds(g * NS, NS)])
            for zz in range(NS):
                s = g * NS + zz
                total = own[s, mine]
                for k in range(NX - 1):
                    total = total + x_in[k, s].astype(jnp.float32)
                y_own[g, zz] = total
                y_out[g, zz] = total.astype(jnp.bfloat16)
        for k in (1, 3, 2):
            send(("b2", k), y_out.at[lax.rem(y + k, NY)], y_in.at[k - 1], at_y(k))

    def b_y_sum():
        for k in (1, 3, 2):
            arrived(("b2", k), y_in.at[k - 1])
        for zz in range(NS):
            total = y_own[y, zz]
            for k in range(NY - 1):
                total = total + y_in[k, zz].astype(jnp.float32)
            z_own[zz] = total
        z_in[z] = z_own[zl]
        for k in range(1, NZ):
            send(("b3", k), z_own.at[lax.rem(zl + k, NS)], z_in.at[z], at_z(k))

    def b_z_sum():
        for k in range(1, NZ):
            arrived(("b3", k), z_in.at[lax.rem(z + NZ - k, NZ)])
        total = z_in[0]
        for k in range(1, NZ):
            total = total + z_in[k]
        gath[me8] = total * FACTOR
        for k in range(1, 8):
            send(("b4", k), gath.at[me8], gath.at[me8], at_8(k))

    def b_write():
        for k in range(1, 8):
            arrived(("b4", k), gath.at[lax.rem(me8 + 8 - k, 8)])
        for p in range(8):
            rows, cols = (p // 2) * PIECE, (p % 2) * CORE
            out_b[rows:rows + PIECE, cols:cols + CORE] = gath[p]

    def a_through():
        def step(s, total):
            for j in (0, 1):
                base = pl.multiple_of(s * CORE + j * UNIT, UNIT)
                total = total + dot_cols(
                    cot[:, pl.ds(base, UNIT)], ubuf[j, lax.div(s, NS), lax.rem(s, NS)]
                )
            return total

        through = lax.fori_loop(0, SHARDS, step, jnp.zeros((CHIP, RANK), jnp.float32)).T
        for core in (0, 1):
            thr[core] = through[:, core * TOK:(core + 1) * TOK]
        send("thr", thr.at[1 - c], thr_in, sibling)

    def a_terms():
        arrived("thr", thr_in)
        total = (thr[c] + thr_in[...]).astype(jnp.bfloat16)
        thr[c] = total.astype(jnp.float32)
        term = jnp.dot(total, latent[...], preferred_element_type=jnp.float32)
        for p in range(8):
            a_own[p] = term[p * 8:(p + 1) * 8]
        for k in range(1, 8):
            send(("a1", k), a_own.at[lax.rem(me8 + k, 8)], a_in.at[k - 1], at_8(k))

    def a_8_sum():
        for k in range(1, 8):
            arrived(("a1", k), a_in.at[k - 1])
        total = a_own[me8]
        for k in range(7):
            total = total + a_in[k]
        ay_in[y] = total
        for k in (1, 3, 2):
            send(("a2", k), ay_in.at[y], ay_in.at[y], at_y(k))

    def a_y_sum():
        for k in (1, 3, 2):
            arrived(("a2", k), ay_in.at[lax.rem(y + NY - k, NY)])
        total = ay_in[0]
        for k in range(1, NY):
            total = total + ay_in[k]
        az_in[z] = total
        for k in range(1, NZ):
            send(("a3", k), az_in.at[z], az_in.at[z], at_z(k))

    def a_z_sum():
        for k in range(1, NZ):
            arrived(("a3", k), az_in.at[lax.rem(z + NZ - k, NZ)])
        total = az_in[0]
        for k in range(1, NZ):
            total = total + az_in[k]
        a_all[me8] = total * FACTOR
        for k in range(1, 8):
            send(("a4", k), a_all.at[me8], a_all.at[me8], at_8(k))

    def a_write():
        for k in range(1, 8):
            arrived(("a4", k), a_all.at[lax.rem(me8 + 8 - k, 8)])
        for p in range(8):
            out_a[p * 8:(p + 1) * 8] = a_all[p]

    def up_wait():
        for j in (0, 1):
            loads["up", j].wait()
        pl.semaphore_wait(barrier, len(partners))

    def take(*pairs):
        for da, db in pairs:
            for j in (0, 1):
                w_take(j, da, db)

    def second(da):
        for j in (0, 1):
            w_second(j, da)

    def use(*pairs):
        for pair in pairs:
            w_ready(*pair)
            w_use(*pair)

    def w_first():
        loads["quant"].wait()
        for j in (0, 1):
            w_start(j)

    up_wait()
    up_start()
    cot_send()
    w_first()
    low_start()
    up_first(-1)
    up_first(1)
    up_first(2)
    second(0)
    b_terms(0)
    b_terms(1)
    take((-1, 0), (1, 0))
    second(-1)
    b_terms(2)
    b_terms(3)
    up_all()
    a_through()
    take((0, -1), (0, 1))
    w_use(0, 0)
    a_terms()
    take((2, 0))
    use((-1, 0), (1, 0))
    b_x_sum()
    second(1)
    take((-1, -1), (-1, 1))
    use((0, -1), (0, 1))
    a_8_sum()
    second(2)
    use((2, 0))
    b_y_sum()
    take((0, 2))
    take((1, -1), (1, 1))
    use((-1, -1), (-1, 1))
    a_y_sum()
    take((-1, 2))
    use((0, 2), (1, -1), (1, 1))
    b_z_sum()
    take((2, -1), (2, 1))
    use((-1, 2))
    a_z_sum()
    take((1, 2))
    use((2, -1), (2, 1))
    b_write()
    take((2, 2))
    use((1, 2))
    w_ready(2, 2)
    w_use(2, 2, others)
    send("acc", acc.at[others], acc_in, sibling)
    w_use(2, 2, tokens)
    acc[tokens] += jnp.dot(
        thr[c].T.astype(jnp.bfloat16), down[...], preferred_element_type=jnp.float32
    )
    a_write()
    arrived("acc", acc_in)
    out_lat[...] = (acc[tokens] + acc_in[...]).astype(jnp.bfloat16)
    for copy in sent:
        copy.wait_send()


def tidy(lat, grad_a, grad_b, out_lat, out_a, out_b):
    out_lat[...] = lat[...]
    out_a[...] = grad_a[...]
    out_b[...] = grad_b[...]


def shards(latent, cotangent, quant, scales, adapter_down, adapter_up):
    vmem = pl.BlockSpec(memory_space=pltpu.VMEM)
    hbm = pl.BlockSpec(memory_space=pl.ANY)
    bf16, f32 = jnp.bfloat16, jnp.float32
    results = (
        jax.ShapeDtypeStruct((TOK, LAT), bf16),
        jax.ShapeDtypeStruct((RANK, LAT), f32),
        jax.ShapeDtypeStruct((RANK, SHARD), f32),
    )
    outs = pl.pallas_call(
        kernel,
        name="adapter_backward",
        out_shape=results,
        in_specs=[pl.BlockSpec(memory_space=pltpu.SMEM)] + [hbm] * 5,
        out_specs=(vmem, vmem, vmem),
        scratch_shapes=[
            pltpu.VMEM((TOK, LAT), bf16),
            pltpu.VMEM((RANK, LAT), bf16),
            pltpu.VMEM((LAT, CORE), bf16),
            pltpu.VMEM((CHIP, MINE), bf16),
            pltpu.VMEM((2, NY, NS, LAT, UNIT), bf16),
            pltpu.VMEM((2, NY, NS, RANK, UNIT), bf16),
            pltpu.VMEM((2, RANK, TOK), bf16),
            pltpu.VMEM((CHIP, LAT), f32),
            pltpu.VMEM((TOK, LAT), f32),
            pltpu.VMEM((2, RANK, TOK), f32),
            pltpu.VMEM((RANK, TOK), f32),
            pltpu.VMEM((SHARDS, RANK, CORE), f32),
            pltpu.VMEM((NX, SHARDS, PIECE, CORE), bf16),
            pltpu.VMEM((NX - 1, SHARDS, PIECE, CORE), bf16),
            pltpu.VMEM((NY, NS, PIECE, CORE), f32),
            pltpu.VMEM((NY, NS, PIECE, CORE), bf16),
            pltpu.VMEM((NY - 1, NS, PIECE, CORE), bf16),
            pltpu.VMEM((NS, PIECE, CORE), f32),
            pltpu.VMEM((NZ, PIECE, CORE), f32),
            pltpu.VMEM((8, PIECE, CORE), f32),
            pltpu.VMEM((8, 8, LAT), f32),
            pltpu.VMEM((7, 8, LAT), f32),
            pltpu.VMEM((NY, 8, LAT), f32),
            pltpu.VMEM((NZ, 8, LAT), f32),
            pltpu.VMEM((8, 8, LAT), f32),
            pltpu.SemaphoreType.DMA((5 + SHARDS,)),
            pltpu.SemaphoreType.DMA((SENDS,)),
            pltpu.SemaphoreType.DMA((RECVS,)),
        ],
        compiler_params=pltpu.CompilerParams(
            collective_id=0, has_side_effects=True, vmem_limit_bytes=56 * 2**20
        ),
        cost_estimate=pl.CostEstimate(
            flops=2 * TOK * COLS * (LAT + 2 * RANK), bytes_accessed=12 * 2**20, transcendentals=0
        ),
    )(scales, latent, cotangent, quant, adapter_down.T, adapter_up)
    lat, grad_a_t, grad_b = pl.pallas_call(
        tidy,
        name="tidy",
        out_shape=results,
        in_specs=[vmem] * 3,
        out_specs=(vmem, vmem, vmem),
    )(*outs)
    return lat, grad_a_t.T, grad_b


def solution(mesh):
    placed = (
        P(("dp", "fsdp"), None),
        P(("dp", "fsdp"), None),
        P(None, "fsdp"),
        P(None, "fsdp"),
        P(),
        P(None, "fsdp"),
    )
    return jax.shard_map(
        shards,
        mesh=mesh,
        in_specs=placed,
        out_specs=(P(("dp", "fsdp"), None), P(), P(None, "fsdp")),
        check_vma=False,
    )
```

time: 95.6 us -> 77.6 us (0.81)
  Pallas kernels: 87.9 us -> 76.8 us
  local copies, waits for them, and re-layouts: 6.51 us -> 0 us
    pallas_call x1 -> x2, Pallas kernels: 87.9 us -> 76.8 us  [the longest x1 74.9 us: shards(): pl.pallas_call(kernel, name='adapter_backward', out_shape=results, in_spe...]
    unnamed x4 -> x0, local copies, waits for them, and re-layouts: 6.51 us -> none
where the time goes in v2:
time: 77.6 us; the launch traced here: 77.4 us
  Pallas kernels  76.8 us (99%)
    pallas_call x1, Pallas kernels, shards(): pl.pallas_call(kernel, name='adapter_backward', out_shape=results, in_spe...  74.9 us
    pallas_call x1, Pallas kernels, shards(): pl.pallas_call(tidy, name='tidy', out_shape=results, in_specs=[vmem] * 3,...  1.94 us

profile of v2, /device:TPU:1, one launch (start us, length us, event | category | flops | bytes accessed | tf_op | source)
XLA Modules:
  0.0 77.4 jit_solution(293797160445980596)
XLA Ops:
  0.6 74.9 %adapter_backward.1 = (bf16[256,512]{1,0:T(8,128)(2,1)}, f32[64,512]{1,0:T(8,128)}, f32[64,1024]{1,0:T(8,128)}) custom-call(f32[4,8]{1,0:T(4,128)} %scales.1, bf16[256,512]{1,0:T(8,128)(2,1)} %latent_hbm.1, bf16[256,16384]{1,0:T(8,128)(2,1)} %cot_hbm.1, bf16[512,1024]{1,0:T(8,128)(2,1)} %quant_hbm.1, bf16[64,512]{1,0:T(8,128)(2,1)} %bitcast.3, ...), custom_call_target="tpu_custom_call" | custom-call | flops 5368709120 | bytes 12582912 | tf_op jit(solution)/shard_map/adapter_backward/pallas_call | solution.py:459
  75.5 1.9 %tidy.1 = (bf16[256,512]{1,0:T(8,128)(2,1)}, f32[64,512]{1,0:T(8,128)}, f32[64,1024]{1,0:T(8,128)}) custom-call(bf16[256,512]{1,0:T(8,128)(2,1)} %get-tuple-element.9.lat, f32[64,512]{1,0:T(8,128)} %get-tuple-element.10.grad_a, f32[64,1024]{1,0:T(8,128)} %get-tuple-element.11.grad_b), custom_call_target="tpu_custom_call" | custom-call | tf_op jit(solution)/shard_map/tidy/pallas_call | solution.py:502

commit v3 on v2

--- a/solution.py
+++ b/solution.py
@@ -21,8 +21,8 @@
 FETCH = LAT - EXCL
 HALF0 = FETCH // 32 * 16
 FACTOR = 1.0 / 65536.0 ** 0.5
-SENDS = 192
-RECVS = 192
+SENDS = 208
+RECVS = 208
 
 ORDER = [
     (-1, 0), (1, 0), (0, -1), (0, 1), (2, 0),
@@ -127,9 +127,10 @@
     def along(j, axis, step):
         return at_y(step) if (j == 0) == (axis == 0) else at_z(step)
 
-    def up_ref(j, da, db):
+    def up_ref(j, da, db, part=None):
         ys, zs = slot(j, da, db)
-        return ubuf.at[j, ys, zs]
+        ref = ubuf.at[j, ys, zs]
+        return ref if part is None else ref.at[part * (RANK // 2):(part + 1) * (RANK // 2)]
 
     def w_ref(j, da, db, part="fetch"):
         ys, zs = slot(j, da, db)
@@ -145,29 +146,48 @@
             return ref.at[pl.ds(par * FETCH, EXCL)]
         return ref.at[pl.ds((1 - par) * FETCH, EXCL)]
 
-    def pass_up(j, da):
-        for step, name in ((1, -1), (-1, 1), (2, 2)):
-            ref = up_ref(j, da, 0)
-            send(("u", j, da, name), ref, ref, along(j, 1, step))
+    def up_second(j, da):
+        ref = up_ref(j, da, 0)
+        send(("u", j, da, -1), ref, ref, along(j, 1, 1))
+        send(("u", j, da, 1), ref, ref, along(j, 1, -1))
 
     def up_start():
         for j in (0, 1):
-            own_up = up_ref(j, 0, 0)
-            for step, name in ((1, -1), (-1, 1), (2, 2)):
-                send(("u", j, name, 0), own_up, own_up, along(j, 0, step))
-        for j in (0, 1):
-            pass_up(j, 0)
-
-    def up_first(da):
-        for j in (0, 1):
-            arrived(("u", j, da, 0), up_ref(j, da, 0))
-            pass_up(j, da)
+            ref = up_ref(j, 0, 0)
+            send(("u", j, -1, 0), ref, ref, along(j, 0, 1))
+            send(("u", j, 1, 0), ref, ref, along(j, 0, -1))
+        for j in (0, 1):
+            up_second(j, 0)
+
+    def up_pass(j, axis, o, da, name):
+        part = 0 if o == -1 else 1
+        db = 0 if axis == 0 else o
+        ref = up_ref(j, da, db, part)
+        send(name + (part,), ref, ref, along(j, axis, -o))
+
+    def up_first(o):
+        for j in (0, 1):
+            arrived(("u", j, o, 0), up_ref(j, o, 0))
+            up_pass(j, 0, o, o, ("u", j, 2, 0))
+            up_second(j, o)
+
+    def up_far():
+        for j in (0, 1):
+            for part in (0, 1):
+                arrived(("u", j, 2, 0, part), up_ref(j, 2, 0, part))
+            up_second(j, 2)
+
+    def up_turn(da):
+        for o in (-1, 1):
+            for j in (0, 1):
+                arrived(("u", j, da, o), up_ref(j, da, o))
+                up_pass(j, 1, o, da, ("u", j, da, 2))
 
     def up_all():
-        for j in (0, 1):
-            for da in (0, -1, 1, 2):
-                for db in (-1, 1, 2):
-                    arrived(("u", j, da, db), up_ref(j, da, db))
+        for da in (0, -1, 1, 2):
+            for j in (0, 1):
+                for part in (0, 1):
+                    arrived(("u", j, da, 2, part), up_ref(j, da, 2, part))
 
     def w_second(j, da):
         ref = w_ref(j, da, 0)
@@ -197,6 +217,8 @@
             ref = w_ref(j, da, db, "h0" if o == -1 else "h1")
             name = ("w", j, 2, 0) if axis == 0 else ("w", j, da, 2)
             send(name + (0 if o == -1 else 1,), ref, ref, along(j, axis, -o))
+
+    def w_cross(j, da, db):
         ref = w_ref(j, da, db, "mine")
         send(("wx", j, da, db), ref, ref, at_x(1 if j == 0 else -1))
 
@@ -276,7 +298,7 @@
             total = y_own[y, zz]
             for k in range(NY - 1):
                 total = total + y_in[k, zz].astype(jnp.float32)
-            z_own[zz] = total
+            z_own[zz] = total.astype(jnp.bfloat16)
         z_in[z] = z_own[zl]
         for k in range(1, NZ):
             send(("b3", k), z_own.at[lax.rem(zl + k, NS)], z_in.at[z], at_z(k))
@@ -284,9 +306,9 @@
     def b_z_sum():
         for k in range(1, NZ):
             arrived(("b3", k), z_in.at[lax.rem(z + NZ - k, NZ)])
-        total = z_in[0]
+        total = z_in[0].astype(jnp.float32)
         for k in range(1, NZ):
-            total = total + z_in[k]
+            total = total + z_in[k].astype(jnp.float32)
         gath[me8] = total * FACTOR
         for k in range(1, 8):
             send(("b4", k), gath.at[me8], gath.at[me8], at_8(k))
@@ -303,11 +325,11 @@
             for j in (0, 1):
                 base = pl.multiple_of(s * CORE + j * UNIT, UNIT)
                 total = total + dot_cols(
-                    cot[:, pl.ds(base, UNIT)], ubuf[j, lax.div(s, NS), lax.rem(s, NS)]
+                    ubuf[j, lax.div(s, NS), lax.rem(s, NS)], cot[:, pl.ds(base, UNIT)]
                 )
             return total
 
-        through = lax.fori_loop(0, SHARDS, step, jnp.zeros((CHIP, RANK), jnp.float32)).T
+        through = lax.fori_loop(0, SHARDS, step, jnp.zeros((RANK, CHIP), jnp.float32), unroll=4)
         for core in (0, 1):
             thr[core] = through[:, core * TOK:(core + 1) * TOK]
         send("thr", thr.at[1 - c], thr_in, sibling)
@@ -318,7 +340,8 @@
         thr[c] = total.astype(jnp.float32)
         term = jnp.dot(total, latent[...], preferred_element_type=jnp.float32)
         for p in range(8):
-            a_own[p] = term[p * 8:(p + 1) * 8]
+            rows, cols = (p // 2) * PIECE, (p % 2) * (LAT // 2)
+            a_own[p] = term[rows:rows + PIECE, cols:cols + LAT // 2]
         for k in range(1, 8):
             send(("a1", k), a_own.at[lax.rem(me8 + k, 8)], a_in.at[k - 1], at_8(k))
 
@@ -338,16 +361,16 @@
         total = ay_in[0]
         for k in range(1, NY):
             total = total + ay_in[k]
-        az_in[z] = total
+        az_in[z] = total.astype(jnp.bfloat16)
         for k in range(1, NZ):
             send(("a3", k), az_in.at[z], az_in.at[z], at_z(k))
 
     def a_z_sum():
         for k in range(1, NZ):
             arrived(("a3", k), az_in.at[lax.rem(z + NZ - k, NZ)])
-        total = az_in[0]
+        total = az_in[0].astype(jnp.float32)
         for k in range(1, NZ):
-            total = total + az_in[k]
+            total = total + az_in[k].astype(jnp.float32)
         a_all[me8] = total * FACTOR
         for k in range(1, 8):
             send(("a4", k), a_all.at[me8], a_all.at[me8], at_8(k))
@@ -356,26 +379,30 @@
         for k in range(1, 8):
             arrived(("a4", k), a_all.at[lax.rem(me8 + 8 - k, 8)])
         for p in range(8):
-            out_a[p * 8:(p + 1) * 8] = a_all[p]
+            rows, cols = (p // 2) * PIECE, (p % 2) * (LAT // 2)
+            out_a[rows:rows + PIECE, cols:cols + LAT // 2] = a_all[p]
 
     def up_wait():
         for j in (0, 1):
             loads["up", j].wait()
         pl.semaphore_wait(barrier, len(partners))
 
-    def take(*pairs):
-        for da, db in pairs:
-            for j in (0, 1):
-                w_take(j, da, db)
+    def take(da, db):
+        for j in (0, 1):
+            w_take(j, da, db)
+
+    def cross(da, db):
+        for j in (0, 1):
+            w_cross(j, da, db)
 
     def second(da):
         for j in (0, 1):
             w_second(j, da)
 
-    def use(*pairs):
-        for pair in pairs:
-            w_ready(*pair)
-            w_use(*pair)
+    def use(da, db):
+        if (da, db) != (0, 0):
+            w_ready(da, db)
+        w_use(da, db)
 
     def w_first():
         loads["quant"].wait()
@@ -383,50 +410,80 @@
             w_start(j)
 
     up_wait()
+    low_start()
     up_start()
     cot_send()
     w_first()
-    low_start()
+    second(0)
     up_first(-1)
+    b_terms(0)
+    take(-1, 0)
     up_first(1)
-    up_first(2)
-    second(0)
-    b_terms(0)
+    take(1, 0)
+    cross(-1, 0)
     b_terms(1)
-    take((-1, 0), (1, 0))
     second(-1)
+    take(0, -1)
     b_terms(2)
+    cross(0, -1)
+    take(0, 1)
     b_terms(3)
+    take(2, 0)
+    up_far()
+    cross(1, 0)
+    take(-1, 1)
+    up_turn(0)
+    take(-1, -1)
+    cross(-1, -1)
+    up_turn(1)
+    take(0, 2)
+    up_turn(-1)
+    cross(0, 1)
+    up_turn(2)
+    cross(0, 2)
+    second(1)
+    cross(2, 0)
+    use(0, 0)
+    cross(-1, 1)
+    b_x_sum()
+    second(2)
+    take(-1, 2)
     up_all()
     a_through()
-    take((0, -1), (0, 1))
-    w_use(0, 0)
+    cross(-1, 2)
     a_terms()
-    take((2, 0))
-    use((-1, 0), (1, 0))
-    b_x_sum()
-    second(1)
-    take((-1, -1), (-1, 1))
-    use((0, -1), (0, 1))
+    take(1, -1)
+    use(0, 1)
+    cross(1, -1)
+    take(1, 1)
+    cross(1, 1)
+    b_y_sum()
+    use(-1, 2)
     a_8_sum()
-    second(2)
-    use((2, 0))
-    b_y_sum()
-    take((0, 2))
-    take((1, -1), (1, 1))
-    use((-1, -1), (-1, 1))
+    take(2, 1)
+    take(2, -1)
+    cross(2, 1)
+    use(0, 2)
+    cross(2, -1)
+    use(1, -1)
+    take(1, 2)
+    cross(1, 2)
     a_y_sum()
-    take((-1, 2))
-    use((0, 2), (1, -1), (1, 1))
     b_z_sum()
-    take((2, -1), (2, 1))
-    use((-1, 2))
+    use(2, 0)
+    take(2, 2)
+    use(0, -1)
+    use(-1, 1)
+    cross(2, 2)
+    use(2, -1)
+    use(-1, 0)
+    use(2, 1)
+    use(1, 1)
     a_z_sum()
-    take((1, 2))
-    use((2, -1), (2, 1))
+    use(1, 2)
+    use(-1, -1)
+    use(1, 0)
     b_write()
-    take((2, 2))
-    use((1, 2))
     w_ready(2, 2)
     w_use(2, 2, others)
     send("acc", acc.at[others], acc_in, sibling)
@@ -480,14 +537,14 @@
             pltpu.VMEM((NY, NS, PIECE, CORE), f32),
             pltpu.VMEM((NY, NS, PIECE, CORE), bf16),
             pltpu.VMEM((NY - 1, NS, PIECE, CORE), bf16),
-            pltpu.VMEM((NS, PIECE, CORE), f32),
-            pltpu.VMEM((NZ, PIECE, CORE), f32),
+            pltpu.VMEM((NS, PIECE, CORE), bf16),
+            pltpu.VMEM((NZ, PIECE, CORE), bf16),
             pltpu.VMEM((8, PIECE, CORE), f32),
-            pltpu.VMEM((8, 8, LAT), f32),
-            pltpu.VMEM((7, 8, LAT), f32),
-            pltpu.VMEM((NY, 8, LAT), f32),
-            pltpu.VMEM((NZ, 8, LAT), f32),
-            pltpu.VMEM((8, 8, LAT), f32),
+            pltpu.VMEM((8, PIECE, LAT // 2), f32),
+            pltpu.VMEM((7, PIECE, LAT // 2), f32),
+            pltpu.VMEM((NY, PIECE, LAT // 2), f32),
+            pltpu.VMEM((NZ, PIECE, LAT // 2), bf16),
+            pltpu.VMEM((8, PIECE, LAT // 2), f32),
             pltpu.SemaphoreType.DMA((5 + SHARDS,)),
             pltpu.SemaphoreType.DMA((SENDS,)),
             pltpu.SemaphoreType.DMA((RECVS,)),

time: 77.6 us -> 70.1 us (0.903)
  Pallas kernels: 76.8 us -> 69.3 us
    pallas_call x1, Pallas kernels: 74.9 us -> 67.4 us  [shards(): pl.pallas_call(kernel, name='adapter_backward', out_shape=results, in_spe...]
where the time goes in v3:
time: 70.1 us; the launch traced here: 70 us
  Pallas kernels  69.3 us (99%)
    pallas_call x1, Pallas kernels, shards(): pl.pallas_call(kernel, name='adapter_backward', out_shape=results, in_spe...  67.4 us
    pallas_call x1, Pallas kernels, shards(): pl.pallas_call(tidy, name='tidy', out_shape=results, in_specs=[vmem] * 3,...  1.94 us

profile of v3, /device:TPU:1, one launch (start us, length us, event | category | flops | bytes accessed | tf_op | source)
XLA Modules:
  0.0 70.0 jit_solution(13736647893340040826)
XLA Ops:
  0.6 67.4 %adapter_backward.1 = (bf16[256,512]{1,0:T(8,128)(2,1)}, f32[64,512]{1,0:T(8,128)}, f32[64,1024]{1,0:T(8,128)}) custom-call(f32[4,8]{1,0:T(4,128)} %scales.1, bf16[256,512]{1,0:T(8,128)(2,1)} %latent_hbm.1, bf16[256,16384]{1,0:T(8,128)(2,1)} %cot_hbm.1, bf16[512,1024]{1,0:T(8,128)(2,1)} %quant_hbm.1, bf16[64,512]{1,0:T(8,128)(2,1)} %bitcast.3, ...), custom_call_target="tpu_custom_call" | custom-call | flops 5368709120 | bytes 12582912 | tf_op jit(solution)/shard_map/adapter_backward/pallas_call | solution.py:516
  68.0 1.9 %tidy.1 = (bf16[256,512]{1,0:T(8,128)(2,1)}, f32[64,512]{1,0:T(8,128)}, f32[64,1024]{1,0:T(8,128)}) custom-call(bf16[256,512]{1,0:T(8,128)(2,1)} %get-tuple-element.9.lat, f32[64,512]{1,0:T(8,128)} %get-tuple-element.10.grad_a, f32[64,1024]{1,0:T(8,128)} %get-tuple-element.11.grad_b), custom_call_target="tpu_custom_call" | custom-call | tf_op jit(solution)/shard_map/tidy/pallas_call | solution.py:559

commit v4 on v3

--- a/solution.py
+++ b/solution.py
@@ -17,7 +17,7 @@
 MINE = COLS // 2
 CHIP = 2 * TOK
 PIECE = RANK // NX
-EXCL = 144
+EXCL = 160
 FETCH = LAT - EXCL
 HALF0 = FETCH // 32 * 16
 FACTOR = 1.0 / 65536.0 ** 0.5
@@ -38,12 +38,12 @@
 
 
 def kernel(
-    scales, latent_hbm, cot_hbm, quant_hbm, down_hbm, up_hbm,
+    scales_hbm, latent_hbm, cot_hbm, quant_hbm, down_hbm, up_hbm,
     out_lat, out_a, out_b,
-    latent, down, quant, cot, wbuf, ubuf, low_t, acc, acc_in, thr, thr_in, own, x_out, x_in,
+    latent, down, quant, cot, wbuf, ubuf, low_t, acc, acc_out, acc_in, thr, thr_in, own, x_out, x_in,
     y_own, y_out, y_in, z_own, z_in, gath,
     a_own, a_in, ay_in, az_in, a_all,
-    load_sem, send_sem, recv_sem,
+    scales, load_sem, send_sem, recv_sem,
 ):
     d, f = lax.axis_index("dp"), lax.axis_index("fsdp")
     x, c = lax.div(d, 4), lax.rem(d, 2)
@@ -112,6 +112,7 @@
     for j in (0, 1):
         load(("up", j), up_hbm.at[:, pl.ds(half + j * UNIT, UNIT)], ubuf.at[j, y, zl])
     load("quant", quant_hbm.at[:, pl.ds(half, CORE)], quant)
+    load("scales", scales_hbm, scales)
     load("latent", latent_hbm, latent)
     load("down", down_hbm, down)
     for s in range(SHARDS):
@@ -142,6 +143,10 @@
             return ref.at[pl.ds(low, HALF0)]
         if part == "h1":
             return ref.at[pl.ds(low + HALF0, FETCH - HALF0)]
+        if part == "top":
+            return ref.at[pl.ds(0, LAT // 2)]
+        if part == "bottom":
+            return ref.at[pl.ds(LAT // 2, LAT // 2)]
         if part == "mine":
             return ref.at[pl.ds(par * FETCH, EXCL)]
         return ref.at[pl.ds((1 - par) * FETCH, EXCL)]
@@ -207,16 +212,22 @@
         send(("w", j, 1, 0), ref, ref, along(j, 0, -1))
 
     def w_take(j, da, db):
-        if db == 2 or (da, db) == (2, 0):
+        if (da, db) == (2, 0):
             arrived(("w", j, da, db, 0), w_ref(j, da, db, "h0"))
             arrived(("w", j, da, db, 1), w_ref(j, da, db, "h1"))
+        elif db == 2:
+            arrived(("w", j, da, db, 0), w_ref(j, da, db, "top"))
+            arrived(("w", j, da, db, 1), w_ref(j, da, db, "bottom"))
         else:
             arrived(("w", j, da, db), w_ref(j, da, db))
-        axis, o = (0, da) if db == 0 else (1, db)
-        if o in (-1, 1):
-            ref = w_ref(j, da, db, "h0" if o == -1 else "h1")
-            name = ("w", j, 2, 0) if axis == 0 else ("w", j, da, 2)
-            send(name + (0 if o == -1 else 1,), ref, ref, along(j, axis, -o))
+        if db == 0 and da != 2:
+            ref = w_ref(j, da, db, "h0" if da == -1 else "h1")
+            send(("w", j, 2, 0, 0 if da == -1 else 1), ref, ref, along(j, 0, -da))
+
+    def w_pass(j, da, db):
+        arrived(("wx", j, da, db), w_ref(j, da, db, "missing"))
+        ref = w_ref(j, da, db, "top" if db == -1 else "bottom")
+        send(("w", j, da, 2, 0 if db == -1 else 1), ref, ref, along(j, 1, -db))
 
     def w_cross(j, da, db):
         ref = w_ref(j, da, db, "mine")
@@ -224,7 +235,8 @@
 
     def w_ready(da, db):
         for j in (0, 1):
-            arrived(("wx", j, da, db), w_ref(j, da, db, "missing"))
+            if db == 0:
+                arrived(("wx", j, da, db), w_ref(j, da, db, "missing"))
 
     def w_use(da, db, rows=slice(None)):
         total = None
@@ -399,6 +411,10 @@
         for j in (0, 1):
             w_second(j, da)
 
+    def onward(da, db):
+        for j in (0, 1):
+            w_pass(j, da, db)
+
     def use(da, db):
         if (da, db) != (0, 0):
             w_ready(da, db)
@@ -406,6 +422,7 @@
 
     def w_first():
         loads["quant"].wait()
+        loads["scales"].wait()
         for j in (0, 1):
             w_start(j)
 
@@ -414,86 +431,90 @@
     up_start()
     cot_send()
     w_first()
+    up_first(-1)
     second(0)
-    up_first(-1)
+    up_first(1)
     b_terms(0)
     take(-1, 0)
-    up_first(1)
-    take(1, 0)
     cross(-1, 0)
     b_terms(1)
-    second(-1)
+    take(1, 0)
+    b_terms(2)
+    take(0, 1)
     take(0, -1)
-    b_terms(2)
-    cross(0, -1)
-    take(0, 1)
+    second(1)
+    up_far()
+    up_turn(1)
+    up_turn(-1)
     b_terms(3)
     take(2, 0)
-    up_far()
-    cross(1, 0)
-    take(-1, 1)
+    second(-1)
     up_turn(0)
-    take(-1, -1)
-    cross(-1, -1)
-    up_turn(1)
-    take(0, 2)
-    up_turn(-1)
+    take(1, -1)
     cross(0, 1)
     up_turn(2)
-    cross(0, 2)
-    second(1)
+    take(1, 1)
+    use(0, 0)
+    cross(0, -1)
+    b_x_sum()
+    cross(1, -1)
+    cross(1, 1)
+    second(2)
+    use(-1, 0)
+    onward(0, -1)
+    cross(1, 0)
+    onward(0, 1)
+    take(-1, 1)
+    use(0, -1)
     cross(2, 0)
-    use(0, 0)
-    cross(-1, 1)
-    b_x_sum()
-    second(2)
-    take(-1, 2)
     up_all()
     a_through()
-    cross(-1, 2)
+    cross(-1, 1)
+    take(-1, -1)
+    b_y_sum()
+    onward(1, -1)
     a_terms()
-    take(1, -1)
+    take(2, 1)
+    cross(-1, -1)
+    take(2, -1)
+    cross(2, -1)
     use(0, 1)
-    cross(1, -1)
-    take(1, 1)
-    cross(1, 1)
-    b_y_sum()
+    cross(2, 1)
+    onward(1, 1)
+    take(0, 2)
+    use(2, 0)
+    use(1, 0)
+    a_8_sum()
+    onward(-1, 1)
+    b_z_sum()
+    onward(-1, -1)
+    use(-1, -1)
+    use(-1, 1)
+    take(1, 2)
+    a_y_sum()
+    onward(2, -1)
+    onward(2, 1)
+    use(2, -1)
+    use(1, 1)
+    use(2, 1)
+    use(0, 2)
+    use(1, 2)
+    take(-1, 2)
+    use(1, -1)
     use(-1, 2)
-    a_8_sum()
-    take(2, 1)
-    take(2, -1)
-    cross(2, 1)
-    use(0, 2)
-    cross(2, -1)
-    use(1, -1)
-    take(1, 2)
-    cross(1, 2)
-    a_y_sum()
-    b_z_sum()
-    use(2, 0)
+    a_z_sum()
     take(2, 2)
-    use(0, -1)
-    use(-1, 1)
-    cross(2, 2)
-    use(2, -1)
-    use(-1, 0)
-    use(2, 1)
-    use(1, 1)
-    a_z_sum()
-    use(1, 2)
-    use(-1, -1)
-    use(1, 0)
     b_write()
-    w_ready(2, 2)
     w_use(2, 2, others)
-    send("acc", acc.at[others], acc_in, sibling)
+    acc_out[...] = acc[others].astype(jnp.bfloat16)
+    send("acc", acc_out, acc_in, sibling)
     w_use(2, 2, tokens)
     acc[tokens] += jnp.dot(
         thr[c].T.astype(jnp.bfloat16), down[...], preferred_element_type=jnp.float32
     )
     a_write()
     arrived("acc", acc_in)
-    out_lat[...] = (acc[tokens] + acc_in[...]).astype(jnp.bfloat16)
+    out_lat[...] = (acc[tokens] + acc_in[...].astype(jnp.float32)).astype(jnp.bfloat16)
     for copy in sent:
         copy.wait_send()
 
@@ -517,7 +538,7 @@
         kernel,
         name="adapter_backward",
         out_shape=results,
-        in_specs=[pl.BlockSpec(memory_space=pltpu.SMEM)] + [hbm] * 5,
+        in_specs=[hbm] * 6,
         out_specs=(vmem, vmem, vmem),
         scratch_shapes=[
             pltpu.VMEM((TOK, LAT), bf16),
@@ -528,7 +549,8 @@
             pltpu.VMEM((2, NY, NS, RANK, UNIT), bf16),
             pltpu.VMEM((2, RANK, TOK), bf16),
             pltpu.VMEM((CHIP, LAT), f32),
-            pltpu.VMEM((TOK, LAT), f32),
+            pltpu.VMEM((TOK, LAT), bf16),
+            pltpu.VMEM((TOK, LAT), bf16),
             pltpu.VMEM((2, RANK, TOK), f32),
             pltpu.VMEM((RANK, TOK), f32),
             pltpu.VMEM((SHARDS, RANK, CORE), f32),
@@ -545,7 +567,8 @@
             pltpu.VMEM((NY, PIECE, LAT // 2), f32),
             pltpu.VMEM((NZ, PIECE, LAT // 2), bf16),
             pltpu.VMEM((8, PIECE, LAT // 2), f32),
-            pltpu.SemaphoreType.DMA((5 + SHARDS,)),
+            pltpu.SMEM((LAT // BLOCK, SHARD // BLOCK), f32),
+            pltpu.SemaphoreType.DMA((6 + SHARDS,)),
             pltpu.SemaphoreType.DMA((SENDS,)),
             pltpu.SemaphoreType.DMA((RECVS,)),
         ],

time: 70.1 us -> 68.2 us (0.973)
  Pallas kernels: 69.3 us -> 67.5 us
    pallas_call x1, Pallas kernels: 67.4 us -> 65.5 us  [shards(): pl.pallas_call(kernel, name='adapter_backward', out_shape=results, in_spe...]
where the time goes in v4:
time: 68.2 us; the launch traced here: 68.1 us
  Pallas kernels  67.5 us (99%)
    pallas_call x1, Pallas kernels, shards(): pl.pallas_call(kernel, name='adapter_backward', out_shape=results, in_spe...  65.5 us
    pallas_call x1, Pallas kernels, shards(): pl.pallas_call(tidy, name='tidy', out_shape=results, in_specs=[vmem] * 3,...  1.94 us

profile of v4, /device:TPU:1, one launch (start us, length us, event | category | flops | bytes accessed | tf_op | source)
XLA Modules:
  0.0 68.1 jit_solution(5428933162957846509)
XLA Ops:
  0.6 65.5 %adapter_backward.1 = (bf16[256,512]{1,0:T(8,128)(2,1)}, f32[64,512]{1,0:T(8,128)}, f32[64,1024]{1,0:T(8,128)}) custom-call(f32[4,8]{1,0:T(4,128)} %scales_hbm.1, bf16[256,512]{1,0:T(8,128)(2,1)} %latent_hbm.1, bf16[256,16384]{1,0:T(8,128)(2,1)} %cot_hbm.1, bf16[512,1024]{1,0:T(8,128)(2,1)} %quant_hbm.1, bf16[64,512]{1,0:T(8,128)(2,1)} %bitcast.3, ...), custom_call_target="tpu_custom_call" | custom-call | flops 5368709120 | bytes 12582912 | tf_op jit(solution)/shard_map/adapter_backward/pallas_call | solution.py:537
  66.2 1.9 %tidy.1 = (bf16[256,512]{1,0:T(8,128)(2,1)}, f32[64,512]{1,0:T(8,128)}, f32[64,1024]{1,0:T(8,128)}) custom-call(bf16[256,512]{1,0:T(8,128)(2,1)} %get-tuple-element.9.lat, f32[64,512]{1,0:T(8,128)} %get-tuple-element.10.grad_a, f32[64,1024]{1,0:T(8,128)} %get-tuple-element.11.grad_b), custom_call_target="tpu_custom_call" | custom-call | tf_op jit(solution)/shard_map/tidy/pallas_call | solution.py:582

commit v5 on v4

--- a/solution.py
+++ b/solution.py
@@ -43,7 +43,7 @@
     latent, down, quant, cot, wbuf, ubuf, low_t, acc, acc_out, acc_in, thr, thr_in, own, x_out, x_in,
     y_own, y_out, y_in, z_own, z_in, gath,
     a_own, a_in, ay_in, az_in, a_all,
-    scales, load_sem, send_sem, recv_sem,
+    lat_done, a_done, b_done, scales, load_sem, send_sem, recv_sem,
 ):
     d, f = lax.axis_index("dp"), lax.axis_index("fsdp")
     x, c = lax.div(d, 4), lax.rem(d, 2)
@@ -106,6 +106,13 @@
         copy.start()
         loads[name] = copy
 
+    stores = []
+
+    def store(src, dst):
+        copy = pltpu.make_async_copy(src, dst, load_sem.at[6 + SHARDS + len(stores)])
+        copy.start()
+        stores.append(copy)
+
     half = pl.multiple_of(c * CORE, CORE)
     tokens = pl.ds(pl.multiple_of(c * TOK, TOK), TOK)
     others = pl.ds(pl.multiple_of((1 - c) * TOK, TOK), TOK)
@@ -113,7 +120,7 @@
         load(("up", j), up_hbm.at[:, pl.ds(half + j * UNIT, UNIT)], ubuf.at[j, y, zl])
     load("quant", quant_hbm.at[:, pl.ds(half, CORE)], quant)
     load("scales", scales_hbm, scales)
-    load("latent", latent_hbm, latent)
+    load("latent", latent_hbm, latent.at[tokens])
     load("down", down_hbm, down)
     for s in range(SHARDS):
         load(
@@ -189,7 +196,7 @@
                 up_pass(j, 1, o, da, ("u", j, da, 2))
 
     def up_all():
-        for da in (0, -1, 1, 2):
+        for da in (-1, 1, 2, 0):
             for j in (0, 1):
                 for part in (0, 1):
                     arrived(("u", j, da, 2, part), up_ref(j, da, 2, part))
@@ -254,11 +261,12 @@
         loads["latent"].wait()
         loads["down"].wait()
         low = jnp.dot(
-            latent[...], down[...].astype(jnp.float32).T.astype(jnp.bfloat16),
+            latent[tokens], down[...].astype(jnp.float32).T.astype(jnp.bfloat16),
             preferred_element_type=jnp.float32,
         )
         low_t[c] = low.astype(jnp.bfloat16).astype(jnp.float32).T.astype(jnp.bfloat16)
         send("low", low_t.at[c], low_t.at[c], sibling)
+        send("latent", latent.at[tokens], latent.at[tokens], sibling)
 
     def cot_send():
         for s in range(SHARDS):
@@ -330,27 +338,34 @@
             arrived(("b4", k), gath.at[lax.rem(me8 + 8 - k, 8)])
         for p in range(8):
             rows, cols = (p // 2) * PIECE, (p % 2) * CORE
-            out_b[rows:rows + PIECE, cols:cols + CORE] = gath[p]
-
-    def a_through():
-        def step(s, total):
-            for j in (0, 1):
-                base = pl.multiple_of(s * CORE + j * UNIT, UNIT)
-                total = total + dot_cols(
-                    ubuf[j, lax.div(s, NS), lax.rem(s, NS)], cot[:, pl.ds(base, UNIT)]
-                )
-            return total
-
-        through = lax.fori_loop(0, SHARDS, step, jnp.zeros((RANK, CHIP), jnp.float32), unroll=4)
+            b_done[rows:rows + PIECE, cols:cols + CORE] = gath[p]
+        store(b_done, out_b)
+
+    def a_through(*dbs):
+        total = None
+        for db in dbs:
+            for da in (0, -1, 1, 2):
+                for j in (0, 1):
+                    ys, zs = slot(j, da, db)
+                    base = pl.multiple_of((ys * NS + zs) * CORE + j * UNIT, UNIT)
+                    term = dot_cols(ubuf[j, ys, zs], cot[:, pl.ds(base, UNIT)])
+                    total = term if total is None else total + term
         for core in (0, 1):
-            thr[core] = through[:, core * TOK:(core + 1) * TOK]
+            part = total[:, core * TOK:(core + 1) * TOK]
+            if 0 in dbs:
+                thr[core] = part
+            else:
+                thr[core] += part
+
+    def a_terms():
+        arrived("latent", latent.at[others])
         send("thr", thr.at[1 - c], thr_in, sibling)
-
-    def a_terms():
-        arrived("thr", thr_in)
-        total = (thr[c] + thr_in[...]).astype(jnp.bfloat16)
-        thr[c] = total.astype(jnp.float32)
-        term = jnp.dot(total, latent[...], preferred_element_type=jnp.float32)
+        term = jnp.dot(
+            thr[0].astype(jnp.bfloat16), latent[:TOK], preferred_element_type=jnp.float32
+        )
+        term += jnp.dot(
+            thr[1].astype(jnp.bfloat16), latent[TOK:], preferred_element_type=jnp.float32
+        )
         for p in range(8):
             rows, cols = (p // 2) * PIECE, (p % 2) * (LAT // 2)
             a_own[p] = term[rows:rows + PIECE, cols:cols + LAT // 2]
@@ -392,7 +407,8 @@
             arrived(("a4", k), a_all.at[lax.rem(me8 + 8 - k, 8)])
         for p in range(8):
             rows, cols = (p // 2) * PIECE, (p % 2) * (LAT // 2)
-            out_a[rows:rows + PIECE, cols:cols + LAT // 2] = a_all[p]
+            a_done[rows:rows + PIECE, cols:cols + LAT // 2] = a_all[p]
+        store(a_done, out_a)
 
     def up_wait():
         for j in (0, 1):
@@ -427,106 +443,117 @@
             w_start(j)
 
     up_wait()
+    up_start()
     low_start()
-    up_start()
+    w_first()
     cot_send()
-    w_first()
+    second(0)
     up_first(-1)
-    second(0)
+    b_terms(0)
+    up_turn(0)
+    take(-1, 0)
     up_first(1)
-    b_terms(0)
-    take(-1, 0)
     cross(-1, 0)
+    second(-1)
     b_terms(1)
+    take(0, -1)
+    take(0, 1)
     take(1, 0)
+    cross(0, -1)
+    up_far()
     b_terms(2)
-    take(0, 1)
-    take(0, -1)
+    up_turn(1)
     second(1)
-    up_far()
-    up_turn(1)
     up_turn(-1)
     b_terms(3)
+    take(-1, 1)
+    a_through(0)
+    up_turn(2)
+    cross(0, 1)
     take(2, 0)
-    second(-1)
-    up_turn(0)
+    cross(-1, 1)
+    second(2)
+    a_through(-1, 1)
     take(1, -1)
-    cross(0, 1)
-    up_turn(2)
+    cross(1, -1)
+    use(0, 0)
+    b_x_sum()
+    up_all()
+    take(-1, -1)
+    onward(0, 1)
+    a_through(2)
     take(1, 1)
-    use(0, 0)
-    cross(0, -1)
-    b_x_sum()
-    cross(1, -1)
+    onward(0, -1)
     cross(1, 1)
-    second(2)
+    a_terms()
+    onward(-1, 1)
+    take(2, 1)
+    use(-1, 1)
+    cross(1, 0)
+    use(0, 1)
+    take(2, -1)
+    cross(-1, -1)
+    cross(2, -1)
+    use(0, -1)
+    onward(1, -1)
+    b_y_sum()
+    take(0, 2)
+    use(1, -1)
+    a_8_sum()
     use(-1, 0)
-    onward(0, -1)
-    cross(1, 0)
-    onward(0, 1)
-    take(-1, 1)
-    use(0, -1)
+    use(0, 2)
+    cross(2, 1)
+    onward(-1, -1)
+    onward(1, 1)
+    use(-1, -1)
+    use(1, 0)
     cross(2, 0)
-    up_all()
-    a_through()
-    cross(-1, 1)
-    take(-1, -1)
-    b_y_sum()
-    onward(1, -1)
-    a_terms()
-    take(2, 1)
-    cross(-1, -1)
-    take(2, -1)
-    cross(2, -1)
-    use(0, 1)
-    cross(2, 1)
-    onward(1, 1)
-    take(0, 2)
-    use(2, 0)
-    use(1, 0)
-    a_8_sum()
-    onward(-1, 1)
+    use(1, 1)
+    a_y_sum()
     b_z_sum()
-    onward(-1, -1)
-    use(-1, -1)
-    use(-1, 1)
-    take(1, 2)
-    a_y_sum()
     onward(2, -1)
     onward(2, 1)
-    use(2, -1)
-    use(1, 1)
-    use(2, 1)
-    use(0, 2)
+    take(1, 2)
     use(1, 2)
     take(-1, 2)
-    use(1, -1)
+    use(2, 0)
+    use(2, 1)
+    use(2, -1)
     use(-1, 2)
     a_z_sum()
+    b_write()
     take(2, 2)
-    b_write()
     w_use(2, 2, others)
     acc_out[...] = acc[others].astype(jnp.bfloat16)
     send("acc", acc_out, acc_in, sibling)
     w_use(2, 2, tokens)
-    acc[tokens] += jnp.dot(
-        thr[c].T.astype(jnp.bfloat16), down[...], preferred_element_type=jnp.float32
-    )
+    arrived("thr", thr_in)
+    through = (thr[c] + thr_in[...]).T.astype(jnp.bfloat16)
+    acc[tokens] += jnp.dot(through, down[...], preferred_element_type=jnp.float32)
     a_write()
     arrived("acc", acc_in)
-    out_lat[...] = (acc[tokens] + acc_in[...].astype(jnp.float32)).astype(jnp.bfloat16)
+    lat_done[...] = (acc[tokens] + acc_in[...].astype(jnp.float32)).astype(jnp.bfloat16)
+    store(lat_done, out_lat)
     for copy in sent:
         copy.wait_send()
-
-
-def tidy(lat, grad_a, grad_b, out_lat, out_a, out_b):
-    out_lat[...] = lat[...]
-    out_a[...] = grad_a[...]
-    out_b[...] = grad_b[...]
+    for copy in stores:
+        copy.wait()
+
+
+def tidy(lat, grad_a, grad_b, out_lat, out_a, out_b, lat_held, a_held, b_held, in_sem, out_sem):
+    moves = ((grad_b, b_held, out_b), (lat, lat_held, out_lat), (grad_a, a_held, out_a))
+    reads = [pltpu.make_async_copy(m[0], m[1], in_sem.at[i]) for i, m in enumerate(moves)]
+    writes = [pltpu.make_async_copy(m[1], m[2], out_sem.at[i]) for i, m in enumerate(moves)]
+    for read in reads:
+        read.start()
+    for read, write in zip(reads, writes):
+        read.wait()
+        write.start()
+    for write in writes:
+        write.wait()
 
 
 def shards(latent, cotangent, quant, scales, adapter_down, adapter_up):
-    vmem = pl.BlockSpec(memory_space=pltpu.VMEM)
     hbm = pl.BlockSpec(memory_space=pl.ANY)
     bf16, f32 = jnp.bfloat16, jnp.float32
     results = (
@@ -539,9 +566,9 @@
         name="adapter_backward",
         out_shape=results,
         in_specs=[hbm] * 6,
-        out_specs=(vmem, vmem, vmem),
+        out_specs=(hbm, hbm, hbm),
         scratch_shapes=[
-            pltpu.VMEM((TOK, LAT), bf16),
+            pltpu.VMEM((CHIP, LAT), bf16),
             pltpu.VMEM((RANK, LAT), bf16),
             pltpu.VMEM((LAT, CORE), bf16),
             pltpu.VMEM((CHIP, MINE), bf16),
@@ -567,8 +594,11 @@
             pltpu.VMEM((NY, PIECE, LAT // 2), f32),
             pltpu.VMEM((NZ, PIECE, LAT // 2), bf16),
             pltpu.VMEM((8, PIECE, LAT // 2), f32),
+            pltpu.VMEM((TOK, LAT), bf16),
+            pltpu.VMEM((RANK, LAT), f32),
+            pltpu.VMEM((RANK, SHARD), f32),
             pltpu.SMEM((LAT // BLOCK, SHARD // BLOCK), f32),
-            pltpu.SemaphoreType.DMA((6 + SHARDS,)),
+            pltpu.SemaphoreType.DMA((9 + SHARDS,)),
             pltpu.SemaphoreType.DMA((SENDS,)),
             pltpu.SemaphoreType.DMA((RECVS,)),
         ],
@@ -583,8 +613,15 @@
         tidy,
         name="tidy",
         out_shape=results,
-        in_specs=[vmem] * 3,
-        out_specs=(vmem, vmem, vmem),
+        in_specs=[hbm] * 3,
+        out_specs=(hbm, hbm, hbm),
+        scratch_shapes=[
+            pltpu.VMEM((TOK, LAT), bf16),
+            pltpu.VMEM((RANK, LAT), f32),
+            pltpu.VMEM((RANK, SHARD), f32),
+            pltpu.SemaphoreType.DMA((3,)),
+            pltpu.SemaphoreType.DMA((3,)),
+        ],
     )(*outs)
     return lat, grad_a_t.T, grad_b
 

time: 68.2 us -> 66.2 us (0.971)
  Pallas kernels: 67.5 us -> 65.4 us
    pallas_call x1, Pallas kernels: 65.5 us -> 63.6 us  [shards(): pl.pallas_call(kernel, name='adapter_backward', out_shape=results, in_spe...]
where the time goes in v5:
time: 66.2 us; the launch traced here: 66.1 us
  Pallas kernels  65.4 us (99%)
    pallas_call x1, Pallas kernels, shards(): pl.pallas_call(kernel, name='adapter_backward', out_shape=results, in_spe...  63.6 us
    pallas_call x1, Pallas kernels, shards(): pl.pallas_call(tidy, name='tidy', out_shape=results, in_specs=[hbm] * 3,...  1.83 us

profile of v5, /device:TPU:1, one launch (start us, length us, event | category | flops | bytes accessed | tf_op | source)
XLA Modules:
  0.0 66.1 jit_solution(2805516977464661594)
XLA Ops:
  0.6 63.6 %adapter_backward.1 = (bf16[256,512]{1,0:T(8,128)(2,1)}, f32[64,512]{1,0:T(8,128)}, f32[64,1024]{1,0:T(8,128)}) custom-call(f32[4,8]{1,0:T(4,128)} %scales_hbm.1, bf16[256,512]{1,0:T(8,128)(2,1)} %latent_hbm.1, bf16[256,16384]{1,0:T(8,128)(2,1)} %cot_hbm.1, bf16[512,1024]{1,0:T(8,128)(2,1)} %quant_hbm.1, bf16[64,512]{1,0:T(8,128)(2,1)} %bitcast.3, ...), custom_call_target="tpu_custom_call" | custom-call | flops 5368709120 | bytes 12582912 | tf_op jit(solution)/shard_map/adapter_backward/pallas_call | solution.py:564
  64.2 1.8 %tidy.1 = (bf16[256,512]{1,0:T(8,128)(2,1)}, f32[64,512]{1,0:T(8,128)}, f32[64,1024]{1,0:T(8,128)}) custom-call(bf16[256,512]{1,0:T(8,128)(2,1)} %get-tuple-element.9.lat, f32[64,512]{1,0:T(8,128)} %get-tuple-element.10.grad_a, f32[64,1024]{1,0:T(8,128)} %get-tuple-element.11.grad_b), custom_call_target="tpu_custom_call" | custom-call | tf_op jit(solution)/shard_map/tidy/pallas_call | solution.py:612

commit v6 on v5

--- a/solution.py
+++ b/solution.py
@@ -21,8 +21,8 @@
 FETCH = LAT - EXCL
 HALF0 = FETCH // 32 * 16
 FACTOR = 1.0 / 65536.0 ** 0.5
-SENDS = 208
-RECVS = 208
+SENDS = 216
+RECVS = 216
 
 ORDER = [
     (-1, 0), (1, 0), (0, -1), (0, 1), (2, 0),
@@ -523,17 +523,24 @@
     a_z_sum()
     b_write()
     take(2, 2)
-    w_use(2, 2, others)
-    acc_out[...] = acc[others].astype(jnp.bfloat16)
-    send("acc", acc_out, acc_in, sibling)
+    strip = TOK // 2
+    for i in (0, 1):
+        rows = pl.ds(pl.multiple_of((1 - c) * TOK + i * strip, strip), strip)
+        part = pl.ds(i * strip, strip)
+        w_use(2, 2, rows)
+        acc_out[part] = acc[rows].astype(jnp.bfloat16)
+        send(("acc", i), acc_out.at[part], acc_in.at[part], sibling)
     w_use(2, 2, tokens)
     arrived("thr", thr_in)
     through = (thr[c] + thr_in[...]).T.astype(jnp.bfloat16)
     acc[tokens] += jnp.dot(through, down[...], preferred_element_type=jnp.float32)
     a_write()
-    arrived("acc", acc_in)
-    lat_done[...] = (acc[tokens] + acc_in[...].astype(jnp.float32)).astype(jnp.bfloat16)
-    store(lat_done, out_lat)
+    for i in (0, 1):
+        rows = pl.ds(pl.multiple_of(c * TOK + i * strip, strip), strip)
+        part = pl.ds(i * strip, strip)
+        arrived(("acc", i), acc_in.at[part])
+        lat_done[part] = (acc[rows] + acc_in[part].astype(jnp.float32)).astype(jnp.bfloat16)
+        store(lat_done.at[part], out_lat.at[part])
     for copy in sent:
         copy.wait_send()
     for copy in stores:
@@ -598,7 +605,7 @@
             pltpu.VMEM((RANK, LAT), f32),
             pltpu.VMEM((RANK, SHARD), f32),
             pltpu.SMEM((LAT // BLOCK, SHARD // BLOCK), f32),
-            pltpu.SemaphoreType.DMA((9 + SHARDS,)),
+            pltpu.SemaphoreType.DMA((10 + SHARDS,)),
             pltpu.SemaphoreType.DMA((SENDS,)),
             pltpu.SemaphoreType.DMA((RECVS,)),
         ],

time: 66.2 us -> 66.3 us (level)
  no operation moved by 1% of the time
where the time goes in v6:
time: 66.3 us; the launch traced here: 66.2 us
  Pallas kernels  65.6 us (99%)
    pallas_call x1, Pallas kernels, shards(): pl.pallas_call(kernel, name='adapter_backward', out_shape=results, in_spe...  63.7 us
    pallas_call x1, Pallas kernels, shards(): pl.pallas_call(tidy, name='tidy', out_shape=results, in_specs=[hbm] * 3,...  1.83 us

profile of v6, /device:TPU:1, one launch (start us, length us, event | category | flops | bytes accessed | tf_op | source)
XLA Modules:
  0.0 66.2 jit_solution(10724212045918390183)
XLA Ops:
  0.6 63.7 %adapter_backward.1 = (bf16[256,512]{1,0:T(8,128)(2,1)}, f32[64,512]{1,0:T(8,128)}, f32[64,1024]{1,0:T(8,128)}) custom-call(f32[4,8]{1,0:T(4,128)} %scales_hbm.1, bf16[256,512]{1,0:T(8,128)(2,1)} %latent_hbm.1, bf16[256,16384]{1,0:T(8,128)(2,1)} %cot_hbm.1, bf16[512,1024]{1,0:T(8,128)(2,1)} %quant_hbm.1, bf16[64,512]{1,0:T(8,128)(2,1)} %bitcast.3, ...), custom_call_target="tpu_custom_call" | custom-call | flops 5368709120 | bytes 12582912 | tf_op jit(solution)/shard_map/adapter_backward/pallas_call | solution.py:571
  64.4 1.8 %tidy.1 = (bf16[256,512]{1,0:T(8,128)(2,1)}, f32[64,512]{1,0:T(8,128)}, f32[64,1024]{1,0:T(8,128)}) custom-call(bf16[256,512]{1,0:T(8,128)(2,1)} %get-tuple-element.9.lat, f32[64,512]{1,0:T(8,128)} %get-tuple-element.10.grad_a, f32[64,1024]{1,0:T(8,128)} %get-tuple-element.11.grad_b), custom_call_target="tpu_custom_call" | custom-call | tf_op jit(solution)/shard_map/tidy/pallas_call | solution.py:619
